TPU v7x, 256 devices: a whole 4x4x8 slice. The times are simulated.
256 devices in a mesh: loop: 64 (over z, x_hi, y), depth: 4 (over x_lo, core).
Axes of the slice: x: 4 (x_hi: 2, x_lo: 2; x = x_hi * 2 + x_lo), y: 4, z: 8, core: 2. Of those that a mesh axis runs over, the one named last changes fastest.
Arguments:
- features: float32 [65536, 128], P(('loop', 'depth')), may hold values from -6 to 6
- norm_scale: float32 [65536], P(('loop', 'depth')), may hold values from 0.03 to 0.3
- weight: bfloat16 [128, 128], replicated, may hold values from -0.5 to 0.5
- cotangent: float32 [65536, 128], P(('loop', 'depth')), may hold values from -6 to 6
- tile_rows: int32 [64, 4, 16, 48], P('loop', 'depth'), may hold values from 0 to 7
- tile_cols: int32 [64, 4, 16, 48], P('loop', 'depth'), may hold values from 0 to 7
- tile_masks: int32 [64, 4, 16, 48, 2048], P('loop', 'depth'), may hold values from 0 to 255, as said below
- tile_counts: int32 [64, 4, 16], P('loop', 'depth'), may hold values from 1 to 48, as said below
Outputs:
- activations: float32 [65536, 128], P(('loop', 'depth'))
- feature_grad: float32 [65536, 128], P(('loop', 'depth'))
- weight_grad: float32 [128, 128], replicated
Inputs may be any that keep to these rules, and one draw needn't show every extreme that they name: `tile_rows`: tile row inside the target block row. `tile_cols`: tile column inside the source block row. `tile_masks`: each word packs 8 entries of a tile row. Slots from tile_counts on are unused. Some block row, member and section uses all 48 slots in every draw.
All inputs are finite; a program needn't handle non-finite values.
Results may differ from a plain program's by a relative error of at most 0.0057.
Values may be sent and summed in bfloat16 or wider, within the bound.
A program may use at most 64 MiB of HBM per device.

v0:
```python
import jax
import jax.numpy as jnp
from jax import lax
from jax.sharding import PartitionSpec as P

TILE = 128
GROUP = 4


def passed_along(block, axis, distance):
    devices = range(lax.axis_size(axis))
    route = [((i - distance) % len(devices), i) for i in devices]
    return lax.ppermute(block, axis, route)


def unpack_bits(words):
    grouped = words.reshape(words.shape[:-1] + (TILE, words.shape[-1] // TILE))
    shifts = jnp.arange(8, dtype=jnp.int32)
    bit_values = jnp.bitwise_and(jnp.right_shift(grouped[..., None], shifts), 1)
    return bit_values.reshape(grouped.shape[:-1] + (grouped.shape[-1] * 8,))


def group_masks(section_words, offset, live_count):
    group_words = lax.dynamic_slice_in_dim(section_words, offset, GROUP, 0)
    live_slots = offset + jnp.arange(GROUP, dtype=jnp.int32) < live_count
    return jnp.where(live_slots[:, None, None], unpack_bits(group_words), 0).astype(jnp.bfloat16)


def forward_section(totals, source, section_id, row_list, col_list, word_list, count_list):
    live_count = count_list[section_id]
    section_rows = row_list[section_id]
    section_cols = col_list[section_id]
    section_words = word_list[section_id]

    def forward_group_step(group_id, running):
        offset = group_id * GROUP
        group_rows = lax.dynamic_slice_in_dim(section_rows, offset, GROUP)
        group_cols = lax.dynamic_slice_in_dim(section_cols, offset, GROUP)
        mask_tiles = group_masks(section_words, offset, live_count)
        picked = jnp.take(source, group_cols, axis=0)
        products = jnp.einsum(
            "gij,gjf->gif", mask_tiles, picked, preferred_element_type=jnp.float32
        )
        return running.at[group_rows].add(products)

    group_count = (live_count + GROUP - 1) // GROUP
    return lax.fori_loop(0, group_count, forward_group_step, totals)


def backward_section(totals, signals, section_id, row_list, col_list, word_list, count_list):
    live_count = count_list[section_id]
    section_rows = row_list[section_id]
    section_cols = col_list[section_id]
    section_words = word_list[section_id]

    def backward_group_step(group_id, running):
        offset = group_id * GROUP
        group_rows = lax.dynamic_slice_in_dim(section_rows, offset, GROUP)
        group_cols = lax.dynamic_slice_in_dim(section_cols, offset, GROUP)
        mask_tiles = group_masks(section_words, offset, live_count)
        picked = jnp.take(signals, group_rows, axis=0)
        products = jnp.einsum(
            "gij,gif->gjf", mask_tiles, picked, preferred_element_type=jnp.float32
        )
        return running.at[group_cols].add(products)

    group_count = (live_count + GROUP - 1) // GROUP
    return lax.fori_loop(0, group_count, backward_group_step, totals)


def per_device(
    features, norm_scale, weight, cotangent, tile_rows, tile_cols, tile_masks, tile_counts
):
    members = lax.axis_size("depth")
    member_id = lax.axis_index("depth")
    row_list = tile_rows[0, 0]
    col_list = tile_cols[0, 0]
    word_list = tile_masks[0, 0]
    count_list = tile_counts[0, 0]
    sections = row_list.shape[0]
    tile_size = TILE
    channels = features.shape[1]

    def forward_at(totals, source, section_id):
        return forward_section(
            totals, source, section_id, row_list, col_list, word_list, count_list
        )

    def backward_at(totals, signals, section_id):
        return backward_section(
            totals, signals, section_id, row_list, col_list, word_list, count_list
        )

    scaled = (norm_scale[:, None] * features).astype(jnp.bfloat16)
    stripe = lax.all_gather(scaled, "depth", axis=0, tiled=True).reshape(-1, tile_size, channels)
    copies = [stripe]
    moved = stripe
    for offset_id in range(members - 1):
        moved = passed_along(moved, "loop", 1)
        copies.append(moved)
    aligned = lax.dynamic_index_in_dim(jnp.stack(copies), member_id, 0, keepdims=False)
    totals = forward_at(jnp.zeros(aligned.shape, jnp.float32), aligned, 0)

    def cycle_step(section_id, carry):
        running, held = carry
        held = passed_along(held, "loop", members)
        return (forward_at(running, held, section_id), held)

    totals, held = lax.fori_loop(1, sections, cycle_step, (totals, aligned))
    summed = lax.psum_scatter(totals, "depth", scatter_dimension=0, tiled=True).reshape(
        -1, channels
    )
    aggregated = norm_scale[:, None] * summed
    aggregated_b = aggregated.astype(jnp.bfloat16)
    pre = jnp.dot(aggregated_b, weight, preferred_element_type=jnp.float32)
    activations = jax.nn.silu(pre)
    sigma = jax.nn.sigmoid(pre)
    signal = (cotangent * (sigma * (1.0 + pre * (1.0 - sigma)))).astype(jnp.bfloat16)
    weight_term = jnp.dot(aggregated_b.T, signal, preferred_element_type=jnp.float32)
    weight_grad = lax.psum(weight_term, ("loop", "depth"))
    backed = jnp.dot(signal, weight.T, preferred_element_type=jnp.float32)
    pushed = (norm_scale[:, None] * backed).astype(jnp.bfloat16)
    signals = lax.all_gather(pushed, "depth", axis=0, tiled=True).reshape(-1, tile_size, channels)
    empty = jnp.zeros(aligned.shape, jnp.float32)
    returned = backward_at(empty, signals, sections - 1)

    def back_step(section_id, running):
        running = passed_along(running, "loop", -members)
        return backward_at(running, signals, sections - 1 - section_id)

    returned = lax.fori_loop(1, sections, back_step, returned)
    partials = [returned]
    carried = returned
    for offset_id in range(members - 1):
        carried = passed_along(carried, "loop", -1)
        partials.append(carried)
    owned = lax.dynamic_index_in_dim(jnp.stack(partials), member_id, 0, keepdims=False)
    gathered = lax.psum_scatter(owned, "depth", scatter_dimension=0, tiled=True).reshape(
        -1, channels
    )
    feature_grad = norm_scale[:, None] * gathered
    return (activations, feature_grad, weight_grad)


def solution(mesh):
    return jax.shard_map(
        per_device,
        mesh=mesh,
        in_specs=(
            P(("loop", "depth"), None),
            P(("loop", "depth")),
            P(),
            P(("loop", "depth"), None),
            P("loop", "depth", None, None),
            P("loop", "depth", None, None),
            P("loop", "depth", None, None, None),
            P("loop", "depth", None),
        ),
        out_specs=(P(("loop", "depth"), None), P(("loop", "depth"), None), P()),
        check_vma=False,
    )
```

profile of v0, /device:TPU:1, one launch (start us, length us, event | category | flops | bytes accessed | tf_op | source)
XLA Modules:
  0.0 1752.2 jit_solution(6163210929640263015)
XLA Ops:
  68.8 563.3 %while.133 = (s32[]{:T(128)}, f32[8,128,128]{2,1,0:T(8,128)S(1)}, bf16[8,128,128]{2,1,0:T(8,128)(2,1)S(1)}, s32[16]{0:T(128)S(1)}, s32[16,48]{1,0:T(8,128)}, /*i...) while((s32[]{:T(128)}, f32[8,128,128]{2,1,0:T(8,128)S(1)}, ...), condition=%wide.region_7.9_spmd, body=%wide.region_3.8_spmd.sunk | while | flops 17171524 | bytes 4038212 | solution.py:109
  72.0 17.3 collective-permute-done.1
  106.8 19.4 %collective-permute-done.1 = bf16[8,128,128]{2,1,0:T(8,128)(2,1)S(1)} collective-permute-done((bf16[8,128,128]{2,1,0:T(8,128)(2,1)S(1)}, bf16[8,128,128]{2,1,0:T(8,128)(2,1)S(1)}, u32[]{:S(2)}, u32[]{:S(2)}) %collective-permute-start.1) | collective-permute-done | bytes 262176 | tf_op jit(solution)/shard_map/while/body/eval_jaxpr/ppermute | solution.py:13
  143.6 23.7 %collective-permute-done.1 = bf16[8,128,128]{2,1,0:T(8,128)(2,1)S(1)} collective-permute-done((bf16[8,128,128]{2,1,0:T(8,128)(2,1)S(1)}, bf16[8,128,128]{2,1,0:T(8,128)(2,1)S(1)}, u32[]{:S(2)}, u32[]{:S(2)}) %collective-permute-start.1) | collective-permute-done | bytes 262176 | tf_op jit(solution)/shard_map/while/body/eval_jaxpr/ppermute | solution.py:13
  358.9 23.2 %collective-permute-start.1 = (bf16[8,128,128]{2,1,0:T(8,128)(2,1)S(1)}, bf16[8,128,128]{2,1,0:T(8,128)(2,1)S(1)}, u32[]{:S(2)}, u32[]{:S(2)}) collective-permute-start(bf16[8,128,128]{2,1,0:T(8,128)(2,1)S(1)} %get-tuple-element.1355), channel_id=1, source_target_pairs={{240,0},{244,4},{248,8},{252,12},{0,16},{4,20},{8,24},{12,28},{16,... | collective-permute-start | bytes 786440 | tf_op jit(solution)/shard_map/while/body/eval_jaxpr/ppermute | solution.py:13
  433.9 23.8 %collective-permute-start.1 = (bf16[8,128,128]{2,1,0:T(8,128)(2,1)S(1)}, bf16[8,128,128]{2,1,0:T(8,128)(2,1)S(1)}, u32[]{:S(2)}, u32[]{:S(2)}) collective-permute-start(bf16[8,128,128]{2,1,0:T(8,128)(2,1)S(1)} %get-tuple-element.1355), channel_id=1, source_target_pairs={{240,0},{244,4},{248,8},{252,12},{0,16},{4,20},{8,24},{12,28},{16,... | collective-permute-start | bytes 786440 | tf_op jit(solution)/shard_map/while/body/eval_jaxpr/ppermute | solution.py:13
  553.2 27.8 %collective-permute-start.1 = (bf16[8,128,128]{2,1,0:T(8,128)(2,1)S(1)}, bf16[8,128,128]{2,1,0:T(8,128)(2,1)S(1)}, u32[]{:S(2)}, u32[]{:S(2)}) collective-permute-start(bf16[8,128,128]{2,1,0:T(8,128)(2,1)S(1)} %get-tuple-element.1355), channel_id=1, source_target_pairs={{240,0},{244,4},{248,8},{252,12},{0,16},{4,20},{8,24},{12,28},{16,... | collective-permute-start | bytes 786440 | tf_op jit(solution)/shard_map/while/body/eval_jaxpr/ppermute | solution.py:13
  596.5 18.0 %collective-permute-start.1 = (bf16[8,128,128]{2,1,0:T(8,128)(2,1)S(1)}, bf16[8,128,128]{2,1,0:T(8,128)(2,1)S(1)}, u32[]{:S(2)}, u32[]{:S(2)}) collective-permute-start(bf16[8,128,128]{2,1,0:T(8,128)(2,1)S(1)} %get-tuple-element.1355), channel_id=1, source_target_pairs={{240,0},{244,4},{248,8},{252,12},{0,16},{4,20},{8,24},{12,28},{16,... | collective-permute-start | bytes 786440 | tf_op jit(solution)/shard_map/while/body/eval_jaxpr/ppermute | solution.py:13
  633.6 104.8 %reduce-scatter.3.cloned.1.call-done = f32[2,128,128]{2,1,0:T(8,128)} async-done(((f32[8,128,128]{2,1,0:T(8,128)}), f32[2,128,128]{2,1,0:T(8,128)}) %reduce-scatter.3.cloned.1.call-update) | async-done | bytes 131088 | tf_op jit(solution)/shard_map/reduce_scatter | solution.py:110
  760.2 613.4 %while.136 = (s32[]{:T(128)}, f32[8,128,128]{2,1,0:T(8,128)S(1)}, s32[16]{0:T(128)S(1)}, s32[16,48]{1,0:T(8,128)}, s32[16,48]{1,0:T(8,128)}, /*index=5*/s32[16,4...) while((s32[]{:T(128)}, f32[8,128,128]{2,1,0:T(8,128)S(1)}, ...), condition=%wide.region_16.18_spmd, body=%wide.region_12.17_spmd.sunk | while | flops 17171524 | bytes 5611088 | solution.py:131
  760.3 21.9 %collective-permute-start = (f32[8,128,128]{2,1,0:T(8,128)S(1)}, f32[8,128,128]{2,1,0:T(8,128)S(1)}, u32[]{:S(2)}, u32[]{:S(2)}) collective-permute-start(f32[8,128,128]{2,1,0:T(8,128)S(1)} %get-tuple-element.1442), channel_id=1, source_target_pairs={{16,0},{20,4},{24,8},{28,12},{32,16},{36,20},{40,24},{44,28},{48,3... | collective-permute-start | bytes 1572872 | tf_op jit(solution)/shard_map/while/body/eval_jaxpr/ppermute | solution.py:13
  799.1 24.5 %collective-permute-start = (f32[8,128,128]{2,1,0:T(8,128)S(1)}, f32[8,128,128]{2,1,0:T(8,128)S(1)}, u32[]{:S(2)}, u32[]{:S(2)}) collective-permute-start(f32[8,128,128]{2,1,0:T(8,128)S(1)} %get-tuple-element.1442), channel_id=1, source_target_pairs={{16,0},{20,4},{24,8},{28,12},{32,16},{36,20},{40,24},{44,28},{48,3... | collective-permute-start | bytes 1572872 | tf_op jit(solution)/shard_map/while/body/eval_jaxpr/ppermute | solution.py:13
  923.3 21.8 %collective-permute-start = (f32[8,128,128]{2,1,0:T(8,128)S(1)}, f32[8,128,128]{2,1,0:T(8,128)S(1)}, u32[]{:S(2)}, u32[]{:S(2)}) collective-permute-start(f32[8,128,128]{2,1,0:T(8,128)S(1)} %get-tuple-element.1442), channel_id=1, source_target_pairs={{16,0},{20,4},{24,8},{28,12},{32,16},{36,20},{40,24},{44,28},{48,3... | collective-permute-start | bytes 1572872 | tf_op jit(solution)/shard_map/while/body/eval_jaxpr/ppermute | solution.py:13
  963.2 24.8 %collective-permute-start = (f32[8,128,128]{2,1,0:T(8,128)S(1)}, f32[8,128,128]{2,1,0:T(8,128)S(1)}, u32[]{:S(2)}, u32[]{:S(2)}) collective-permute-start(f32[8,128,128]{2,1,0:T(8,128)S(1)} %get-tuple-element.1442), channel_id=1, source_target_pairs={{16,0},{20,4},{24,8},{28,12},{32,16},{36,20},{40,24},{44,28},{48,3... | collective-permute-start | bytes 1572872 | tf_op jit(solution)/shard_map/while/body/eval_jaxpr/ppermute | solution.py:13
  1007.8 19.1 %collective-permute-start = (f32[8,128,128]{2,1,0:T(8,128)S(1)}, f32[8,128,128]{2,1,0:T(8,128)S(1)}, u32[]{:S(2)}, u32[]{:S(2)}) collective-permute-start(f32[8,128,128]{2,1,0:T(8,128)S(1)} %get-tuple-element.1442), channel_id=1, source_target_pairs={{16,0},{20,4},{24,8},{28,12},{32,16},{36,20},{40,24},{44,28},{48,3... | collective-permute-start | bytes 1572872 | tf_op jit(solution)/shard_map/while/body/eval_jaxpr/ppermute | solution.py:13
  1043.8 24.5 %collective-permute-start = (f32[8,128,128]{2,1,0:T(8,128)S(1)}, f32[8,128,128]{2,1,0:T(8,128)S(1)}, u32[]{:S(2)}, u32[]{:S(2)}) collective-permute-start(f32[8,128,128]{2,1,0:T(8,128)S(1)} %get-tuple-element.1442), channel_id=1, source_target_pairs={{16,0},{20,4},{24,8},{28,12},{32,16},{36,20},{40,24},{44,28},{48,3... | collective-permute-start | bytes 1572872 | tf_op jit(solution)/shard_map/while/body/eval_jaxpr/ppermute | solution.py:13
  1090.6 19.1 %collective-permute-start = (f32[8,128,128]{2,1,0:T(8,128)S(1)}, f32[8,128,128]{2,1,0:T(8,128)S(1)}, u32[]{:S(2)}, u32[]{:S(2)}) collective-permute-start(f32[8,128,128]{2,1,0:T(8,128)S(1)} %get-tuple-element.1442), channel_id=1, source_target_pairs={{16,0},{20,4},{24,8},{28,12},{32,16},{36,20},{40,24},{44,28},{48,3... | collective-permute-start | bytes 1572872 | tf_op jit(solution)/shard_map/while/body/eval_jaxpr/ppermute | solution.py:13
  1129.3 21.8 %collective-permute-start = (f32[8,128,128]{2,1,0:T(8,128)S(1)}, f32[8,128,128]{2,1,0:T(8,128)S(1)}, u32[]{:S(2)}, u32[]{:S(2)}) collective-permute-start(f32[8,128,128]{2,1,0:T(8,128)S(1)} %get-tuple-element.1442), channel_id=1, source_target_pairs={{16,0},{20,4},{24,8},{28,12},{32,16},{36,20},{40,24},{44,28},{48,3... | collective-permute-start | bytes 1572872 | tf_op jit(solution)/shard_map/while/body/eval_jaxpr/ppermute | solution.py:13
  1165.3 27.2 %collective-permute-start = (f32[8,128,128]{2,1,0:T(8,128)S(1)}, f32[8,128,128]{2,1,0:T(8,128)S(1)}, u32[]{:S(2)}, u32[]{:S(2)}) collective-permute-start(f32[8,128,128]{2,1,0:T(8,128)S(1)} %get-tuple-element.1442), channel_id=1, source_target_pairs={{16,0},{20,4},{24,8},{28,12},{32,16},{36,20},{40,24},{44,28},{48,3... | collective-permute-start | bytes 1572872 | tf_op jit(solution)/shard_map/while/body/eval_jaxpr/ppermute | solution.py:13
  1245.0 21.8 %collective-permute-start = (f32[8,128,128]{2,1,0:T(8,128)S(1)}, f32[8,128,128]{2,1,0:T(8,128)S(1)}, u32[]{:S(2)}, u32[]{:S(2)}) collective-permute-start(f32[8,128,128]{2,1,0:T(8,128)S(1)} %get-tuple-element.1442), channel_id=1, source_target_pairs={{16,0},{20,4},{24,8},{28,12},{32,16},{36,20},{40,24},{44,28},{48,3... | collective-permute-start | bytes 1572872 | tf_op jit(solution)/shard_map/while/body/eval_jaxpr/ppermute | solution.py:13
  1290.5 24.8 %collective-permute-start = (f32[8,128,128]{2,1,0:T(8,128)S(1)}, f32[8,128,128]{2,1,0:T(8,128)S(1)}, u32[]{:S(2)}, u32[]{:S(2)}) collective-permute-start(f32[8,128,128]{2,1,0:T(8,128)S(1)} %get-tuple-element.1442), channel_id=1, source_target_pairs={{16,0},{20,4},{24,8},{28,12},{32,16},{36,20},{40,24},{44,28},{48,3... | collective-permute-start | bytes 1572872 | tf_op jit(solution)/shard_map/while/body/eval_jaxpr/ppermute | solution.py:13
  1334.9 21.8 %collective-permute-start = (f32[8,128,128]{2,1,0:T(8,128)S(1)}, f32[8,128,128]{2,1,0:T(8,128)S(1)}, u32[]{:S(2)}, u32[]{:S(2)}) collective-permute-start(f32[8,128,128]{2,1,0:T(8,128)S(1)} %get-tuple-element.1442), channel_id=1, source_target_pairs={{16,0},{20,4},{24,8},{28,12},{32,16},{36,20},{40,24},{44,28},{48,3... | collective-permute-start | bytes 1572872 | tf_op jit(solution)/shard_map/while/body/eval_jaxpr/ppermute | solution.py:13
  1413.3 86.2 %reduce-scatter.5.cloned.1.call-done = f32[2,128,128]{2,1,0:T(8,128)} async-done(((f32[8,128,128]{2,1,0:T(8,128)}), f32[2,128,128]{2,1,0:T(8,128)}) %reduce-scatter.5.cloned.1.call-update) | async-done | bytes 131088 | tf_op jit(solution)/shard_map/reduce_scatter | solution.py:138
  1501.1 243.0 %all-reduce.2.cloned.1.call-done = f32[128,128]{1,0:T(8,128)} async-done(((f32[128,128]{1,0:T(8,128)}), f32[128,128]{1,0:T(8,128)}) %all-reduce.2.cloned.1.call-update) | async-done | bytes 65552 | tf_op jit(solution)/shard_map/psum | solution.py:120
  (1931 shorter events, 1274.7 us)
Async XLA Ops:
  7.2 731.2 %reduce-scatter.3.cloned.1.call-start = ((), (), s32[]{:S(2)}) async-start(), calls=%async_computation.2 | async-start | bytes 655360 | tf_op jit(solution)/shard_map/reduce_scatter | solution.py:110
  103.6 22.5 %collective-permute-start.1 = (bf16[8,128,128]{2,1,0:T(8,128)(2,1)S(1)}, bf16[8,128,128]{2,1,0:T(8,128)(2,1)S(1)}, u32[]{:S(2)}, u32[]{:S(2)}) collective-permute-start(bf16[8,128,128]{2,1,0:T(8,128)(2,1)S(1)} %get-tuple-element.1355), channel_id=1, source_target_pairs={{240,0},{244,4},{248,8},{252,12},{0,16},{4,20},{8,24},{12,28},{16,... | collective-permute-start | bytes 786440 | tf_op jit(solution)/shard_map/while/body/eval_jaxpr/ppermute | solution.py:13
  140.5 26.8 %collective-permute-start.1 = (bf16[8,128,128]{2,1,0:T(8,128)(2,1)S(1)}, bf16[8,128,128]{2,1,0:T(8,128)(2,1)S(1)}, u32[]{:S(2)}, u32[]{:S(2)}) collective-permute-start(bf16[8,128,128]{2,1,0:T(8,128)(2,1)S(1)} %get-tuple-element.1355), channel_id=1, source_target_pairs={{240,0},{244,4},{248,8},{252,12},{0,16},{4,20},{8,24},{12,28},{16,... | collective-permute-start | bytes 786440 | tf_op jit(solution)/shard_map/while/body/eval_jaxpr/ppermute | solution.py:13
  175.9 24.0 %collective-permute-start.1 = (bf16[8,128,128]{2,1,0:T(8,128)(2,1)S(1)}, bf16[8,128,128]{2,1,0:T(8,128)(2,1)S(1)}, u32[]{:S(2)}, u32[]{:S(2)}) collective-permute-start(bf16[8,128,128]{2,1,0:T(8,128)(2,1)S(1)} %get-tuple-element.1355), channel_id=1, source_target_pairs={{240,0},{244,4},{248,8},{252,12},{0,16},{4,20},{8,24},{12,28},{16,... | collective-permute-start | bytes 786440 | tf_op jit(solution)/shard_map/while/body/eval_jaxpr/ppermute | solution.py:13
  241.1 30.4 %collective-permute-start.1 = (bf16[8,128,128]{2,1,0:T(8,128)(2,1)S(1)}, bf16[8,128,128]{2,1,0:T(8,128)(2,1)S(1)}, u32[]{:S(2)}, u32[]{:S(2)}) collective-permute-start(bf16[8,128,128]{2,1,0:T(8,128)(2,1)S(1)} %get-tuple-element.1355), channel_id=1, source_target_pairs={{240,0},{244,4},{248,8},{252,12},{0,16},{4,20},{8,24},{12,28},{16,... | collective-permute-start | bytes 786440 | tf_op jit(solution)/shard_map/while/body/eval_jaxpr/ppermute | solution.py:13
  285.9 24.4 %collective-permute-start.1 = (bf16[8,128,128]{2,1,0:T(8,128)(2,1)S(1)}, bf16[8,128,128]{2,1,0:T(8,128)(2,1)S(1)}, u32[]{:S(2)}, u32[]{:S(2)}) collective-permute-start(bf16[8,128,128]{2,1,0:T(8,128)(2,1)S(1)} %get-tuple-element.1355), channel_id=1, source_target_pairs={{240,0},{244,4},{248,8},{252,12},{0,16},{4,20},{8,24},{12,28},{16,... | collective-permute-start | bytes 786440 | tf_op jit(solution)/shard_map/while/body/eval_jaxpr/ppermute | solution.py:13
  358.9 27.4 %collective-permute-start.1 = (bf16[8,128,128]{2,1,0:T(8,128)(2,1)S(1)}, bf16[8,128,128]{2,1,0:T(8,128)(2,1)S(1)}, u32[]{:S(2)}, u32[]{:S(2)}) collective-permute-start(bf16[8,128,128]{2,1,0:T(8,128)(2,1)S(1)} %get-tuple-element.1355), channel_id=1, source_target_pairs={{240,0},{244,4},{248,8},{252,12},{0,16},{4,20},{8,24},{12,28},{16,... | collective-permute-start | bytes 786440 | tf_op jit(solution)/shard_map/while/body/eval_jaxpr/ppermute | solution.py:13
  433.9 29.4 %collective-permute-start.1 = (bf16[8,128,128]{2,1,0:T(8,128)(2,1)S(1)}, bf16[8,128,128]{2,1,0:T(8,128)(2,1)S(1)}, u32[]{:S(2)}, u32[]{:S(2)}) collective-permute-start(bf16[8,128,128]{2,1,0:T(8,128)(2,1)S(1)} %get-tuple-element.1355), channel_id=1, source_target_pairs={{240,0},{244,4},{248,8},{252,12},{0,16},{4,20},{8,24},{12,28},{16,... | collective-permute-start | bytes 786440 | tf_op jit(solution)/shard_map/while/body/eval_jaxpr/ppermute | solution.py:13
  553.2 31.8 %collective-permute-start.1 = (bf16[8,128,128]{2,1,0:T(8,128)(2,1)S(1)}, bf16[8,128,128]{2,1,0:T(8,128)(2,1)S(1)}, u32[]{:S(2)}, u32[]{:S(2)}) collective-permute-start(bf16[8,128,128]{2,1,0:T(8,128)(2,1)S(1)} %get-tuple-element.1355), channel_id=1, source_target_pairs={{240,0},{244,4},{248,8},{252,12},{0,16},{4,20},{8,24},{12,28},{16,... | collective-permute-start | bytes 786440 | tf_op jit(solution)/shard_map/while/body/eval_jaxpr/ppermute | solution.py:13
  633.0 866.5 %reduce-scatter.5.cloned.1.call-start = ((), (), s32[]{:S(2)}) async-start(), calls=%async_computation.3 | async-start | bytes 655360 | tf_op jit(solution)/shard_map/reduce_scatter | solution.py:138
  760.3 28.0 %collective-permute-start = (f32[8,128,128]{2,1,0:T(8,128)S(1)}, f32[8,128,128]{2,1,0:T(8,128)S(1)}, u32[]{:S(2)}, u32[]{:S(2)}) collective-permute-start(f32[8,128,128]{2,1,0:T(8,128)S(1)} %get-tuple-element.1442), channel_id=1, source_target_pairs={{16,0},{20,4},{24,8},{28,12},{32,16},{36,20},{40,24},{44,28},{48,3... | collective-permute-start | bytes 1572872 | tf_op jit(solution)/shard_map/while/body/eval_jaxpr/ppermute | solution.py:13
  799.1 30.6 %collective-permute-start = (f32[8,128,128]{2,1,0:T(8,128)S(1)}, f32[8,128,128]{2,1,0:T(8,128)S(1)}, u32[]{:S(2)}, u32[]{:S(2)}) collective-permute-start(f32[8,128,128]{2,1,0:T(8,128)S(1)} %get-tuple-element.1442), channel_id=1, source_target_pairs={{16,0},{20,4},{24,8},{28,12},{32,16},{36,20},{40,24},{44,28},{48,3... | collective-permute-start | bytes 1572872 | tf_op jit(solution)/shard_map/while/body/eval_jaxpr/ppermute | solution.py:13
  884.6 22.5 %collective-permute-start = (f32[8,128,128]{2,1,0:T(8,128)S(1)}, f32[8,128,128]{2,1,0:T(8,128)S(1)}, u32[]{:S(2)}, u32[]{:S(2)}) collective-permute-start(f32[8,128,128]{2,1,0:T(8,128)S(1)} %get-tuple-element.1442), channel_id=1, source_target_pairs={{16,0},{20,4},{24,8},{28,12},{32,16},{36,20},{40,24},{44,28},{48,3... | collective-permute-start | bytes 1572872 | tf_op jit(solution)/shard_map/while/body/eval_jaxpr/ppermute | solution.py:13
  923.3 29.1 %collective-permute-start = (f32[8,128,128]{2,1,0:T(8,128)S(1)}, f32[8,128,128]{2,1,0:T(8,128)S(1)}, u32[]{:S(2)}, u32[]{:S(2)}) collective-permute-start(f32[8,128,128]{2,1,0:T(8,128)S(1)} %get-tuple-element.1442), channel_id=1, source_target_pairs={{16,0},{20,4},{24,8},{28,12},{32,16},{36,20},{40,24},{44,28},{48,3... | collective-permute-start | bytes 1572872 | tf_op jit(solution)/shard_map/while/body/eval_jaxpr/ppermute | solution.py:13
  963.2 31.0 %collective-permute-start = (f32[8,128,128]{2,1,0:T(8,128)S(1)}, f32[8,128,128]{2,1,0:T(8,128)S(1)}, u32[]{:S(2)}, u32[]{:S(2)}) collective-permute-start(f32[8,128,128]{2,1,0:T(8,128)S(1)} %get-tuple-element.1442), channel_id=1, source_target_pairs={{16,0},{20,4},{24,8},{28,12},{32,16},{36,20},{40,24},{44,28},{48,3... | collective-permute-start | bytes 1572872 | tf_op jit(solution)/shard_map/while/body/eval_jaxpr/ppermute | solution.py:13
  1007.8 25.2 %collective-permute-start = (f32[8,128,128]{2,1,0:T(8,128)S(1)}, f32[8,128,128]{2,1,0:T(8,128)S(1)}, u32[]{:S(2)}, u32[]{:S(2)}) collective-permute-start(f32[8,128,128]{2,1,0:T(8,128)S(1)} %get-tuple-element.1442), channel_id=1, source_target_pairs={{16,0},{20,4},{24,8},{28,12},{32,16},{36,20},{40,24},{44,28},{48,3... | collective-permute-start | bytes 1572872 | tf_op jit(solution)/shard_map/while/body/eval_jaxpr/ppermute | solution.py:13
  1043.8 30.6 %collective-permute-start = (f32[8,128,128]{2,1,0:T(8,128)S(1)}, f32[8,128,128]{2,1,0:T(8,128)S(1)}, u32[]{:S(2)}, u32[]{:S(2)}) collective-permute-start(f32[8,128,128]{2,1,0:T(8,128)S(1)} %get-tuple-element.1442), channel_id=1, source_target_pairs={{16,0},{20,4},{24,8},{28,12},{32,16},{36,20},{40,24},{44,28},{48,3... | collective-permute-start | bytes 1572872 | tf_op jit(solution)/shard_map/while/body/eval_jaxpr/ppermute | solution.py:13
  1090.6 25.2 %collective-permute-start = (f32[8,128,128]{2,1,0:T(8,128)S(1)}, f32[8,128,128]{2,1,0:T(8,128)S(1)}, u32[]{:S(2)}, u32[]{:S(2)}) collective-permute-start(f32[8,128,128]{2,1,0:T(8,128)S(1)} %get-tuple-element.1442), channel_id=1, source_target_pairs={{16,0},{20,4},{24,8},{28,12},{32,16},{36,20},{40,24},{44,28},{48,3... | collective-permute-start | bytes 1572872 | tf_op jit(solution)/shard_map/while/body/eval_jaxpr/ppermute | solution.py:13
  1129.3 27.9 %collective-permute-start = (f32[8,128,128]{2,1,0:T(8,128)S(1)}, f32[8,128,128]{2,1,0:T(8,128)S(1)}, u32[]{:S(2)}, u32[]{:S(2)}) collective-permute-start(f32[8,128,128]{2,1,0:T(8,128)S(1)} %get-tuple-element.1442), channel_id=1, source_target_pairs={{16,0},{20,4},{24,8},{28,12},{32,16},{36,20},{40,24},{44,28},{48,3... | collective-permute-start | bytes 1572872 | tf_op jit(solution)/shard_map/while/body/eval_jaxpr/ppermute | solution.py:13
  1165.3 35.5 %collective-permute-start = (f32[8,128,128]{2,1,0:T(8,128)S(1)}, f32[8,128,128]{2,1,0:T(8,128)S(1)}, u32[]{:S(2)}, u32[]{:S(2)}) collective-permute-start(f32[8,128,128]{2,1,0:T(8,128)S(1)} %get-tuple-element.1442), channel_id=1, source_target_pairs={{16,0},{20,4},{24,8},{28,12},{32,16},{36,20},{40,24},{44,28},{48,3... | collective-permute-start | bytes 1572872 | tf_op jit(solution)/shard_map/while/body/eval_jaxpr/ppermute | solution.py:13
  1245.0 32.0 %collective-permute-start = (f32[8,128,128]{2,1,0:T(8,128)S(1)}, f32[8,128,128]{2,1,0:T(8,128)S(1)}, u32[]{:S(2)}, u32[]{:S(2)}) collective-permute-start(f32[8,128,128]{2,1,0:T(8,128)S(1)} %get-tuple-element.1442), channel_id=1, source_target_pairs={{16,0},{20,4},{24,8},{28,12},{32,16},{36,20},{40,24},{44,28},{48,3... | collective-permute-start | bytes 1572872 | tf_op jit(solution)/shard_map/while/body/eval_jaxpr/ppermute | solution.py:13
  1290.5 30.9 %collective-permute-start = (f32[8,128,128]{2,1,0:T(8,128)S(1)}, f32[8,128,128]{2,1,0:T(8,128)S(1)}, u32[]{:S(2)}, u32[]{:S(2)}) collective-permute-start(f32[8,128,128]{2,1,0:T(8,128)S(1)} %get-tuple-element.1442), channel_id=1, source_target_pairs={{16,0},{20,4},{24,8},{28,12},{32,16},{36,20},{40,24},{44,28},{48,3... | collective-permute-start | bytes 1572872 | tf_op jit(solution)/shard_map/while/body/eval_jaxpr/ppermute | solution.py:13
  1334.9 27.9 %collective-permute-start = (f32[8,128,128]{2,1,0:T(8,128)S(1)}, f32[8,128,128]{2,1,0:T(8,128)S(1)}, u32[]{:S(2)}, u32[]{:S(2)}) collective-permute-start(f32[8,128,128]{2,1,0:T(8,128)S(1)} %get-tuple-element.1442), channel_id=1, source_target_pairs={{16,0},{20,4},{24,8},{28,12},{32,16},{36,20},{40,24},{44,28},{48,3... | collective-permute-start | bytes 1572872 | tf_op jit(solution)/shard_map/while/body/eval_jaxpr/ppermute | solution.py:13
  1412.4 331.8 %all-reduce.2.cloned.1.call-start = ((), (), s32[]{:S(2)}) async-start(), calls=%async_computation.4 | async-start | bytes 131072 | tf_op jit(solution)/shard_map/psum | solution.py:120
  (20 other events, 2342.2 us)
Sparse Core Ops, SparseCore 0:
  633.1 105.3 reduce-scatter.2
  1412.5 86.9 reduce-scatter.4
  1505.6 238.5 all-reduce.1
where the time goes:
time: 1760 us; the launch traced here: 1750 us
  waiting for transfers between devices  691 us (39%)
  starting transfers between devices  501 us (28%)
  other arithmetic  238 us (14%)
  local copies, waits for them, and re-layouts  217 us (12%)
  matrix products  45.6 us (3%)
  loops' own time  29.9 us (2%)
    ppermute x36, starting transfers between devices, passed_along(): return lax.ppermute(block, axis, route)  501 us
    ppermute x36, waiting for transfers between devices, passed_along(): return lax.ppermute(block, axis, route)  257 us
    psum x1, waiting for transfers between devices, per_device(): weight_grad = lax.psum(weight_term, ('loop', 'depth'))  243 us
    reduce_scatter x1, waiting for transfers between devices, per_device(): lax.psum_scatter(totals, 'depth', scatter_dimension=0, tiled=True)  105 us
    reduce_scatter x1, waiting for transfers between devices, per_device(): lax.psum_scatter(owned, 'depth', scatter_dimension=0, tiled=True)  86.2 us
    scatter-add x77, other arithmetic, backward_group_step(): return running.at[group_cols].add(products)  57.7 us
    scatter-add x77, other arithmetic, forward_group_step(): return running.at[group_rows].add(products)  57.6 us
    and x77, other arithmetic, forward_group_step(): picked = jnp.take(source, group_cols, axis=0)  56 us
  transfers between devices with their start and end apart: 39, of which 39 were waited for; matrix products, arithmetic and copies ran while one was open for 4% of the time, Pallas kernels for 0%

commit v1 on v0

v1 whole, which is shorter than its diff:
```python
import functools

import jax
import jax.numpy as jnp
from jax import lax
from jax.experimental import pallas as pl
from jax.experimental.pallas import tpu as pltpu
from jax.sharding import PartitionSpec as P

TILE = 128
SECTIONS = 16
CAP = 48
STRIPE = 1024
PIECE = 256
FEAT = 128
RING = 8
UNROLL = 4
MESH = pl.DeviceIdType.MESH


def dense_kernel(rows, cols, counts, words, out, packed):
    section = pl.program_id(0)
    live_count = counts[section]
    out[...] = jnp.zeros_like(out)
    for eight in range(CAP // 8):
        slots = pl.ds(eight * 8, 8)
        for part in range(4):
            value = words[0, slots, pl.ds(part * 512, 128)]
            for step in range(1, 4):
                value = value | (words[0, slots, pl.ds(part * 512 + step * 128, 128)] << (8 * step))
            packed[slots, part, :] = value
    lane = lax.broadcasted_iota(jnp.int32, (8, 128), 1)
    row = lax.broadcasted_iota(jnp.int32, (8, 128), 0)
    place = row * 16 + lax.rem(lane, 16)
    bit = lax.div(lane, 16)

    def tile_of(slot):
        live = jnp.where(slot < live_count, 1, 0)
        strips = []
        for part in range(4):
            spread = jnp.broadcast_to(packed[slot, pl.ds(part, 1), :], (8, 128))
            near = jnp.take_along_axis(spread, place, axis=1, mode="promise_in_bounds")
            for step in range(4):
                strips.append(((near >> (bit + 8 * step)) & live).astype(jnp.float32))
        return jnp.concatenate(strips, axis=0).astype(jnp.bfloat16)

    def group_step(group, carry):
        tiles = [tile_of(group * UNROLL + index) for index in range(UNROLL)]
        for index in range(UNROLL):
            slot = group * UNROLL + index
            top = pl.multiple_of(rows[section, slot] * TILE, TILE)
            left = pl.multiple_of(cols[section, slot] * TILE, TILE)
            out[0, pl.ds(top, TILE), pl.ds(left, TILE)] += tiles[index]
        return carry

    lax.fori_loop(0, (live_count + UNROLL - 1) // UNROLL, group_step, 0)


def dense_blocks(tile_rows, tile_cols, tile_counts, tile_masks):
    return pl.pallas_call(
        dense_kernel,
        out_shape=jax.ShapeDtypeStruct((SECTIONS, STRIPE, STRIPE), jnp.bfloat16),
        grid_spec=pltpu.PrefetchScalarGridSpec(
            num_scalar_prefetch=3,
            grid=(SECTIONS,),
            in_specs=[pl.BlockSpec((1, CAP, 2048), lambda k, *_: (k, 0, 0))],
            out_specs=pl.BlockSpec((1, STRIPE, STRIPE), lambda k, *_: (k, 0, 0)),
            scratch_shapes=[pltpu.VMEM((CAP, 4, 128), jnp.int32)],
        ),
        compiler_params=pltpu.CompilerParams(vmem_limit_bytes=32 * 1024 * 1024),
        cost_estimate=pl.CostEstimate(flops=50_000_000, bytes_accessed=40_000_000, transcendentals=0),
    )(tile_rows, tile_cols, tile_counts, tile_masks)


def layer_kernel(
    features, norm, weight, cotangent, dense, act, feature_grad, weight_grad,
    blocks, stripes, own, totals, parts, pushed, own_pushed, sums, going, coming, coming_low, shares, shared, terms, other_terms,
    dense_sem, team_send, team_recv, ring_send, ring_send_low, ring_recv, part_send, part_recv, push_send, push_recv,
    back_send, back_recv, back_recv_low, share_send, share_recv, term_send, term_recv,
):
    loop = lax.axis_index("loop")
    depth = lax.axis_index("depth")
    z = loop // 8
    half = (loop // 4) % 2
    y = loop % 4
    node = loop // 4
    kind = (y - depth + 4) % 4
    first = depth == 0

    def remote(source, target, send, recv, device):
        return pltpu.make_async_remote_copy(
            src_ref=source, dst_ref=target, send_sem=send, recv_sem=recv, device_id=device, device_id_type=MESH
        )

    def toggled(value, bit):
        return value + bit - 2 * bit * ((value // bit) % 2)

    above = (((z + 1) % RING) * 8 + loop % 8, depth)
    below = (((z + RING - 1) % RING) * 8 + loop % 8, depth)
    team = [[((z * 2 + other) * 4 + (y + member) % 4, member) for member in range(4)] for other in range(2)]
    owners = [[((z * 2 + other) * 4 + kind, piece) for piece in range(4)] for other in range(2)]
    beside = [(loop, (depth + offset) % 4) for offset in range(1, 4)]
    before = [(depth + 4 - offset) % 4 for offset in range(1, 4)]
    partners = [
        (loop, toggled(depth, 1)), (loop, toggled(depth, 2)), (toggled(loop, 4), depth), (toggled(loop, 1), depth),
        (toggled(loop, 2), depth), (toggled(loop, 8), depth), (toggled(loop, 16), depth), (toggled(loop, 32), depth),
    ]

    def section_of(slot):
        return ((loop - depth - kind - 4 * slot + 128) // 4) % SECTIONS

    def step_of(index):
        distance = (index + 2) // 4
        up = ((index + 2) // 2) % 2
        other = index % 2
        slot = ((z + RING - distance + 2 * distance * up) % RING) * 2 + other
        passes = (index >= 2) & ((distance < 3) | ((distance == 3) & (other == up)))
        return distance, up, other, slot, passes

    def load_of(section):
        return pltpu.make_async_copy(dense.at[section], blocks.at[section], dense_sem.at[section])

    def load_step(index, carry):
        load_of(section_of(step_of(index)[3])).start()
        return carry

    lax.fori_loop(0, SECTIONS, load_step, 0)

    barrier = pltpu.get_barrier_semaphore()
    for device in [above, below] + beside + [partners[2], partners[3], partners[4], partners[6], partners[7]]:
        pl.semaphore_signal(barrier, inc=1, device_id=device, device_id_type=MESH)
    for other in range(2):
        for index in range(4):
            def greet(other=other, index=index):
                pl.semaphore_signal(barrier, inc=1, device_id=team[other][index], device_id_type=MESH)
                pl.semaphore_signal(barrier, inc=1, device_id=owners[other][index], device_id_type=MESH)

            if index == 0:
                pl.when(jnp.logical_not(first & (half == other)))(greet)
            else:
                greet()

    order_row = lax.broadcasted_iota(jnp.int32, (TILE, TILE), 0)
    order_col = lax.broadcasted_iota(jnp.int32, (TILE, TILE), 1)
    order = jnp.where(order_col == 8 * (order_row % 16) + order_row // 16, 1.0, 0.0)
    norm_row = norm[...]
    norm_full = jnp.broadcast_to(norm_row, (FEAT, PIECE)).T
    scaled = (norm_full * features[...]).astype(jnp.bfloat16)
    for tile in range(2):
        own[pl.ds(tile * TILE, TILE), :] = jnp.dot(
            order.astype(jnp.bfloat16), scaled[tile * TILE:(tile + 1) * TILE], preferred_element_type=jnp.float32
        ).astype(jnp.bfloat16)

    pl.semaphore_wait(barrier, jnp.where(first, 24, 26))

    mine = pl.ds(pl.multiple_of(depth * PIECE, PIECE), PIECE)

    def team_copy(other, member):
        return remote(
            own, stripes.at[node, mine], team_send.at[other, member], team_recv.at[half, depth], team[other][member]
        )

    for other in range(2):
        for member in range(4):
            if member == 0:
                @pl.when(jnp.logical_not(first & (half == other)))
                def _(other=other):
                    team_copy(other, 0).start()
            else:
                team_copy(other, member).start()

    @pl.when(first)
    def _():
        stripes[node, 0:PIECE, :] = own[...]

    totals[...] = jnp.zeros_like(totals)

    def ring_up(slot):
        return remote(stripes.at[slot], stripes.at[slot], ring_send.at[slot], ring_recv.at[slot], above)

    def ring_down(slot):
        return remote(stripes.at[slot], stripes.at[slot], ring_send.at[slot], ring_recv.at[slot], below)

    def ring_down_own(slot, other):
        return remote(stripes.at[slot], stripes.at[slot], ring_send_low.at[other], ring_recv.at[slot], below)

    def forward_step(index, carry):
        distance, up, other, slot, passes = step_of(index)
        section = section_of(slot)

        @pl.when(index < 2)
        def _():
            for piece in range(4):
                def arrived(piece=piece):
                    remote(
                        own, stripes.at[slot, pl.ds(piece * PIECE, PIECE)], team_send.at[0, 0],
                        team_recv.at[other, piece], above,
                    ).wait_recv()

                if piece == 0:
                    pl.when(jnp.logical_not(first & (half == other)))(arrived)
                else:
                    arrived()
            ring_up(slot).start()
            ring_down_own(slot, other).start()

        @pl.when(index >= 2)
        def _():
            ring_up(slot).wait_recv()

        @pl.when(passes & (up == 0))
        def _():
            ring_up(slot).start()

        @pl.when(passes & (up == 1))
        def _():
            ring_down(slot).start()

        load_of(section).wait()
        totals[...] += jnp.dot(blocks[section], stripes[slot], preferred_element_type=jnp.float32)
        return carry

    lax.fori_loop(0, SECTIONS, forward_step, 0)

    def part_copy(offset):
        target = pl.ds(pl.multiple_of(beside[offset][1] * PIECE, PIECE), PIECE)
        return remote(
            totals.at[target], parts.at[offset], part_send.at[offset], part_recv.at[offset], beside[offset]
        )

    for offset in range(3):
        part_copy(offset).start()
    summed = totals[mine, :]
    for offset in range(3):
        part_copy(offset).wait_recv()
        summed = summed + parts[offset]

    aggregated_b = (norm_full * summed).astype(jnp.bfloat16)
    pre = jnp.dot(aggregated_b, weight[...], preferred_element_type=jnp.float32)
    sigma = jax.nn.sigmoid(pre)
    act[...] = pre * sigma
    signal = (cotangent[...] * (sigma * (1.0 + pre * (1.0 - sigma)))).astype(jnp.bfloat16)
    backed = lax.dot_general(weight[...], signal, (((1,), (1,)), ((), ())), preferred_element_type=jnp.float32)
    own_pushed[...] = (norm_row * backed).astype(jnp.bfloat16)

    def push_copy(offset):
        return remote(
            own_pushed, pushed.at[:, mine], push_send.at[offset], push_recv.at[offset], beside[offset]
        )

    for offset in range(3):
        push_copy(offset).start()
    pushed[:, mine] = own_pushed[...]
    terms[0] = lax.dot_general(aggregated_b, signal, (((0,), (0,)), ((), ())), preferred_element_type=jnp.float32)

    def term_copy(step):
        return remote(terms.at[step], other_terms.at[step], term_send.at[step], term_recv.at[step], partners[step])

    term_copy(0).start()
    for offset in range(3):
        source = pl.ds(pl.multiple_of(before[offset] * PIECE, PIECE), PIECE)
        remote(
            own_pushed, pushed.at[:, source], push_send.at[offset], push_recv.at[offset], beside[offset]
        ).wait_recv()

    def share_copy(other, piece):
        return remote(
            shares.at[other, piece], shared.at[half, depth], share_send.at[other, piece], share_recv.at[half, depth],
            owners[other][piece],
        )

    def back_arrived(slot):
        return remote(going.at[slot], coming.at[slot], back_send.at[slot], back_recv.at[slot], above)

    def back_arrived_low(slot, other):
        return remote(going.at[slot], coming_low.at[other], back_send.at[slot], back_recv_low.at[other], below)

    def backward_step(count, carry):
        index = SECTIONS - 1 - count
        distance, up, other, slot, passes = step_of(index)
        section = section_of(slot)
        sums[...] = jnp.dot(pushed[...], blocks[section], preferred_element_type=jnp.float32)

        @pl.when(passes | (index < 2))
        def _():
            back_arrived(slot).wait_recv()
            sums[...] += coming[slot].astype(jnp.float32)

        @pl.when(index < 2)
        def _():
            back_arrived_low(slot, other).wait_recv()
            sums[...] += coming_low[other].astype(jnp.float32)
            for piece in range(4):
                shares[other, piece] = sums[:, piece * PIECE:(piece + 1) * PIECE].astype(jnp.bfloat16)

        for which in range(2):
            @pl.when((index < 2) & (other == which))
            def _(which=which):
                for piece in range(4):
                    if piece == 0:
                        @pl.when(jnp.logical_not(first & (half == which)))
                        def _():
                            share_copy(which, 0).start()

                        @pl.when(first & (half == which))
                        def _():
                            shared[half, 0] = shares[which, 0]
                    else:
                        share_copy(which, piece).start()

        @pl.when(index >= 2)
        def _():
            going[slot] = sums[...].astype(jnp.bfloat16)

        last_far = distance == 4

        @pl.when((index >= 2) & (((up == 0) & jnp.logical_not(last_far)) | (last_far & (other == 0))))
        def _():
            remote(going.at[slot], coming.at[slot], back_send.at[slot], back_recv.at[slot], below).start()

        @pl.when((index >= 2) & (((up == 1) & (distance > 1)) | (last_far & (other == 1))))
        def _():
            remote(going.at[slot], coming.at[slot], back_send.at[slot], back_recv.at[slot], above).start()

        @pl.when((index >= 2) & (up == 1) & (distance == 1))
        def _():
            remote(going.at[slot], coming_low.at[other], back_send.at[slot], back_recv_low.at[other], above).start()

        for step in range(1, 8):
            @pl.when(count == 2 * step)
            def _(step=step):
                term_copy(step - 1).wait_recv()
                terms[step] = terms[step - 1] + other_terms[step - 1]
                term_copy(step).start()

        return carry

    lax.fori_loop(0, SECTIONS, backward_step, 0)

    term_copy(7).wait_recv()
    weight_grad[...] = terms[7] + other_terms[7]

    gathered = jnp.zeros((FEAT, PIECE), jnp.float32)
    for other in range(2):
        for member in range(4):
            def share_arrived(other=other, member=member):
                remote(
                    shares.at[0, 0], shared.at[other, member], share_send.at[0, 0], share_recv.at[other, member], above
                ).wait_recv()

            if member == 0:
                pl.when(jnp.logical_not(first & (half == other)))(share_arrived)
            else:
                share_arrived()
            gathered = gathered + shared[other, member].astype(jnp.float32)
    for tile in range(2):
        feature_grad[pl.ds(tile * TILE, TILE), :] = norm_full[tile * TILE:(tile + 1) * TILE] * lax.dot_general(
            order, gathered[:, tile * TILE:(tile + 1) * TILE], (((0,), (1,)), ((), ())),
            precision=lax.Precision.HIGHEST, preferred_element_type=jnp.float32,
        )

    for other in range(2):
        for index in range(4):
            def sent(other=other, index=index):
                team_copy(other, index).wait_send()
                share_copy(other, index).wait_send()

            if index == 0:
                pl.when(jnp.logical_not(first & (half == other)))(sent)
            else:
                sent()
    for offset in range(3):
        part_copy(offset).wait_send()
        push_copy(offset).wait_send()
    for step in range(8):
        term_copy(step).wait_send()

    def sent_step(index, carry):
        distance, up, other, slot, passes = step_of(index)

        @pl.when(index < 2)
        def _():
            ring_down_own(slot, other).wait_send()

        @pl.when(passes | (index < 2))
        def _():
            ring_up(slot).wait_send()

        @pl.when(index >= 2)
        def _():
            back_arrived(slot).wait_send()

        return carry

    lax.fori_loop(0, SECTIONS, sent_step, 0)


def layer(features, norm_row, weight, cotangent, dense):
    vmem = pl.BlockSpec(memory_space=pltpu.VMEM)
    dma = pltpu.SemaphoreType.DMA
    bf16, f32 = jnp.bfloat16, jnp.float32
    return pl.pallas_call(
        layer_kernel,
        out_shape=(
            jax.ShapeDtypeStruct((PIECE, FEAT), f32),
            jax.ShapeDtypeStruct((PIECE, FEAT), f32),
            jax.ShapeDtypeStruct((FEAT, FEAT), f32),
        ),
        in_specs=[vmem, vmem, vmem, vmem, pl.BlockSpec(memory_space=pl.ANY)],
        out_specs=(vmem, vmem, vmem),
        scratch_shapes=[
            pltpu.VMEM((SECTIONS, STRIPE, STRIPE), bf16),
            pltpu.VMEM((SECTIONS, STRIPE, FEAT), bf16),
            pltpu.VMEM((PIECE, FEAT), bf16),
            pltpu.VMEM((STRIPE, FEAT), f32),
            pltpu.VMEM((3, PIECE, FEAT), f32),
            pltpu.VMEM((FEAT, STRIPE), bf16),
            pltpu.VMEM((FEAT, PIECE), bf16),
            pltpu.VMEM((FEAT, STRIPE), f32),
            pltpu.VMEM((SECTIONS, FEAT, STRIPE), bf16),
            pltpu.VMEM((SECTIONS, FEAT, STRIPE), bf16),
            pltpu.VMEM((2, FEAT, STRIPE), bf16),
            pltpu.VMEM((2, 4, FEAT, PIECE), bf16),
            pltpu.VMEM((2, 4, FEAT, PIECE), bf16),
            pltpu.VMEM((8, FEAT, FEAT), f32),
            pltpu.VMEM((8, FEAT, FEAT), f32),
            dma((SECTIONS,)), dma((2, 4)), dma((2, 4)), dma((SECTIONS,)), dma((2,)), dma((SECTIONS,)),
            dma((3,)), dma((3,)), dma((3,)), dma((3,)),
            dma((SECTIONS,)), dma((SECTIONS,)), dma((2,)), dma((2, 4)), dma((2, 4)), dma((8,)), dma((8,)),
        ],
        compiler_params=pltpu.CompilerParams(
            collective_id=0, has_side_effects=True, vmem_limit_bytes=60 * 1024 * 1024
        ),
        cost_estimate=pl.CostEstimate(flops=9_000_000_000, bytes_accessed=34_000_000, transcendentals=32768),
    )(features, norm_row, weight, cotangent, dense)


def per_device(features, norm_scale, weight, cotangent, tile_rows, tile_cols, tile_masks, tile_counts):
    dense = dense_blocks(tile_rows[0, 0], tile_cols[0, 0], tile_counts[0, 0], tile_masks[0, 0])
    return layer(features, norm_scale.reshape(1, -1), weight, cotangent, dense)


def solution(mesh):
    return jax.shard_map(
        per_device,
        mesh=mesh,
        in_specs=(
            P(("loop", "depth"), None),
            P(("loop", "depth")),
            P(),
            P(("loop", "depth"), None),
            P("loop", "depth", None, None),
            P("loop", "depth", None, None),
            P("loop", "depth", None, None, None),
            P("loop", "depth", None),
        ),
        out_specs=(P(("loop", "depth"), None), P(("loop", "depth"), None), P()),
        check_vma=False,
    )
```

time: 1760 us -> 176 us (0.10)
  waiting for transfers between devices: 691 us -> 0 us
  starting transfers between devices: 501 us -> 0 us
  other arithmetic: 238 us -> 0 us
  local copies, waits for them, and re-layouts: 217 us -> 9.43 us
  Pallas kernels: 0 us -> 165 us
  matrix products: 45.6 us -> 0 us
  loops' own time: 29.9 us -> 0 us
    ppermute x36 -> x0, starting transfers between devices: 501 us -> none  [passed_along(): return lax.ppermute(block, axis, route)]
    ppermute x36 -> x0, waiting for transfers between devices: 257 us -> none  [passed_along(): return lax.ppermute(block, axis, route)]
    psum x1 -> x0, waiting for transfers between devices: 243 us -> none  [per_device(): weight_grad = lax.psum(weight_term, ('loop', 'depth'))]
    reduce_scatter x2 -> x0, waiting for transfers between devices: 191 us -> none  [the longest x1 105 us: per_device(): lax.psum_scatter(totals, 'depth', scatter_dimension=0, tiled=True)]
    pallas_call x0 -> x2, Pallas kernels: none -> 165 us  [the longest x1 142 us: layer(): pl.pallas_call(layer_kernel, out_shape=(jax.ShapeDtypeStruct((PIECE, FEAT...]
    scatter-add x154 -> x0, other arithmetic: 115 us -> none  [the longest x77 57.7 us: backward_group_step(): return running.at[group_cols].add(products)]
    and x154 -> x0, other arithmetic: 105 us -> none  [the longest x77 56 us: forward_group_step(): picked = jnp.take(source, group_cols, axis=0)]
    gather x154 -> x0, local copies, waits for them, and re-layouts: 88.1 us -> none  [the longest x77 44.1 us: forward_group_step(): picked = jnp.take(source, group_cols, axis=0)]
  transfers between devices with their start and end apart: 39 -> 0, of which waited for: 39 -> 0; matrix products, arithmetic and copies ran while one was open for 4% -> 0% of each run, Pallas kernels for 0% -> 0%
where the time goes in v1:
time: 176 us; the launch traced here: 175 us
  Pallas kernels  165 us (94%)
  local copies, waits for them, and re-layouts  9.43 us (5%)
    pallas_call x1, Pallas kernels, layer(): pl.pallas_call(layer_kernel, out_shape=(jax.ShapeDtypeStruct((PIECE, FEAT...  142 us
    pallas_call x1, Pallas kernels, dense_blocks(): pl.pallas_call(dense_kernel, out_shape=jax.ShapeDtypeStruct((SECTIONS, ST...  22.8 us
    unnamed x11, local copies, waits for them, and re-layouts  9.43 us

profile of v1, /device:TPU:1, one launch (start us, length us, event | category | flops | bytes accessed | tf_op | source)
XLA Modules:
  0.0 175.3 jit_solution(1222116560311868909)
XLA Ops:
  0.6 0.0 copy-start
  0.6 2.8 %copy-done = s32[1,1,16,48,2048]{4,3,2,1,0:T(8,128)S(1)} copy-done((s32[1,1,16,48,2048]{4,3,2,1,0:T(8,128)S(1)}, s32[1,1,16,48,2048]{4,3,2,1,0:T(8,128)}, u32[]{:S(2)}) %copy-start) | copy-done | bytes 6291480
  3.4 0.0 copy-start.1
  3.4 0.7 copy-done.1
  4.1 0.0 copy-start.2
  4.1 0.7 copy-done.2
  4.8 0.0 copy-start.3
  4.8 0.7 copy-done.3
  5.5 22.8 %shard_map.103.dense = bf16[16,1024,1024]{2,1,0:T(8,128)(2,1)} custom-call(s32[16,48]{1,0:T(8,128)S(1)} %bitcast.6, s32[16,48]{1,0:T(8,128)S(1)} %bitcast.7, s32[16]{0:T(128)S(1)} %bitcast.8, s32[16,48,2048]{2,1,0:T(8,128)S(1)} %bitcast.5), custom_call_target="tpu_custom_call" | custom-call | flops 50000000 | bytes 40000000 | tf_op jit(solution)/shard_map/pallas_call | solution.py:60
  28.3 142.4 %shard_map.104 = (f32[256,128]{1,0:T(8,128)}, f32[256,128]{1,0:T(8,128)}, f32[128,128]{1,0:T(8,128)}) custom-call(f32[256,128]{1,0:T(8,128)} %features.1, f32[1,256]{1,0:T(1,128)} %bitcast.9, bf16[128,128]{1,0:T(8,128)(2,1)} %weight.1, f32[256,128]{1,0:T(8,128)} %cotangent.1, bf16[16,1024,1024]{2,1,0:T(8,128)(2,1)} %shard_map.103.dense), custom_call_target="tpu_custom_call" | custom-call | flops 8999999488 | bytes 34000000 | tf_op jit(solution)/shard_map/pallas_call | solution.py:402
  170.7 1.6 copy.14
  172.3 1.6 copy.15
  173.8 1.5 copy.16
Async XLA Ops:
  0.6 2.8 %copy-start = (s32[1,1,16,48,2048]{4,3,2,1,0:T(8,128)S(1)}, s32[1,1,16,48,2048]{4,3,2,1,0:T(8,128)}, u32[]{:S(2)}) copy-start(s32[1,1,16,48,2048]{4,3,2,1,0:T(8,128)} %param.14) | copy-start | bytes 18874372
  3.4 0.7 copy-start.1
  4.1 0.7 copy-start.2
  4.8 0.7 copy-start.3

commit v2 on v1

--- a/solution.py
+++ b/solution.py
@@ -1,5 +1,3 @@
-import functools
-
 import jax
 import jax.numpy as jnp
 from jax import lax
@@ -15,6 +13,8 @@
 FEAT = 128
 RING = 8
 UNROLL = 4
+WIDE = 512
+LAG = 2
 MESH = pl.DeviceIdType.MESH
 
 
@@ -22,6 +22,7 @@
     section = pl.program_id(0)
     live_count = counts[section]
     out[...] = jnp.zeros_like(out)
+    packed[pl.ds(CAP, UNROLL)] = jnp.zeros((UNROLL, 4, 128), jnp.int32)
     for eight in range(CAP // 8):
         slots = pl.ds(eight * 8, 8)
         for part in range(4):
@@ -34,26 +35,31 @@
     place = row * 16 + lax.rem(lane, 16)
     bit = lax.div(lane, 16)
 
-    def tile_of(slot):
-        live = jnp.where(slot < live_count, 1, 0)
-        strips = []
-        for part in range(4):
-            spread = jnp.broadcast_to(packed[slot, pl.ds(part, 1), :], (8, 128))
-            near = jnp.take_along_axis(spread, place, axis=1, mode="promise_in_bounds")
-            for step in range(4):
-                strips.append(((near >> (bit + 8 * step)) & live).astype(jnp.float32))
-        return jnp.concatenate(strips, axis=0).astype(jnp.bfloat16)
-
-    def group_step(group, carry):
-        tiles = [tile_of(group * UNROLL + index) for index in range(UNROLL)]
+    def near_of(group):
+        return [
+            jnp.take_along_axis(
+                jnp.broadcast_to(packed[group * UNROLL + index, pl.ds(part, 1), :], (8, 128)),
+                place, axis=1, mode="promise_in_bounds",
+            )
+            for index in range(UNROLL) for part in range(4)
+        ]
+
+    def group_step(group, nears):
+        later = near_of(group + 1)
         for index in range(UNROLL):
             slot = group * UNROLL + index
+            live = jnp.where(slot < live_count, 1, 0)
+            strips = [
+                ((nears[4 * index + part] >> (bit + 8 * step)) & live).astype(jnp.float32)
+                for part in range(4) for step in range(4)
+            ]
+            tile = jnp.concatenate(strips, axis=0).astype(jnp.bfloat16)
             top = pl.multiple_of(rows[section, slot] * TILE, TILE)
             left = pl.multiple_of(cols[section, slot] * TILE, TILE)
-            out[0, pl.ds(top, TILE), pl.ds(left, TILE)] += tiles[index]
-        return carry
-
-    lax.fori_loop(0, (live_count + UNROLL - 1) // UNROLL, group_step, 0)
+            out[0, pl.ds(top, TILE), pl.ds(left, TILE)] += tile
+        return later
+
+    lax.fori_loop(0, (live_count + UNROLL - 1) // UNROLL, group_step, near_of(0))
 
 
 def dense_blocks(tile_rows, tile_cols, tile_counts, tile_masks):
@@ -65,18 +71,20 @@
             grid=(SECTIONS,),
             in_specs=[pl.BlockSpec((1, CAP, 2048), lambda k, *_: (k, 0, 0))],
             out_specs=pl.BlockSpec((1, STRIPE, STRIPE), lambda k, *_: (k, 0, 0)),
-            scratch_shapes=[pltpu.VMEM((CAP, 4, 128), jnp.int32)],
+            scratch_shapes=[pltpu.VMEM((CAP + UNROLL, 4, 128), jnp.int32)],
         ),
-        compiler_params=pltpu.CompilerParams(vmem_limit_bytes=32 * 1024 * 1024),
+        compiler_params=pltpu.CompilerParams(vmem_limit_bytes=60 * 1024 * 1024),
         cost_estimate=pl.CostEstimate(flops=50_000_000, bytes_accessed=40_000_000, transcendentals=0),
     )(tile_rows, tile_cols, tile_counts, tile_masks)
 
 
 def layer_kernel(
     features, norm, weight, cotangent, dense, act, feature_grad, weight_grad,
-    blocks, stripes, own, totals, parts, pushed, own_pushed, sums, going, coming, coming_low, shares, shared, terms, other_terms,
-    dense_sem, team_send, team_recv, ring_send, ring_send_low, ring_recv, part_send, part_recv, push_send, push_recv,
-    back_send, back_recv, back_recv_low, share_send, share_recv, term_send, term_recv,
+    blocks, stripes, own, totals, parts, pushed, own_pushed, sums, going, going_thin, coming, coming_thin, coming_low,
+    coming_thin_low, given, taken, shares, shared, terms, other_terms,
+    dense_sem, team_send, team_recv, ring_send, ring_send_low, ring_recv, thin_send, thin_send_low, thin_recv, peer_send,
+    peer_recv, part_send, part_recv, push_send, push_recv, back_send, back_recv, back_recv_low, back_thin_send,
+    back_thin_recv, back_thin_recv_low, give_send, give_recv, share_send, share_recv, term_send, term_recv,
 ):
     loop = lax.axis_index("loop")
     depth = lax.axis_index("depth")
@@ -100,6 +108,8 @@
     team = [[((z * 2 + other) * 4 + (y + member) % 4, member) for member in range(4)] for other in range(2)]
     owners = [[((z * 2 + other) * 4 + kind, piece) for piece in range(4)] for other in range(2)]
     beside = [(loop, (depth + offset) % 4) for offset in range(1, 4)]
+    peers = [(depth + offset) % 4 for offset in range(1, 4)]
+    peer_devices = [(node * 4 + (kind + member) % 4, member) for member in peers]
     before = [(depth + 4 - offset) % 4 for offset in range(1, 4)]
     partners = [
         (loop, toggled(depth, 1)), (loop, toggled(depth, 2)), (toggled(loop, 4), depth), (toggled(loop, 1), depth),
@@ -127,7 +137,7 @@
     lax.fori_loop(0, SECTIONS, load_step, 0)
 
     barrier = pltpu.get_barrier_semaphore()
-    for device in [above, below] + beside + [partners[2], partners[3], partners[4], partners[6], partners[7]]:
+    for device in [above, below] + beside + peer_devices + [partners[2], partners[3], partners[4], partners[6], partners[7]]:
         pl.semaphore_signal(barrier, inc=1, device_id=device, device_id_type=MESH)
     for other in range(2):
         for index in range(4):
@@ -151,7 +161,7 @@
             order.astype(jnp.bfloat16), scaled[tile * TILE:(tile + 1) * TILE], preferred_element_type=jnp.float32
         ).astype(jnp.bfloat16)
 
-    pl.semaphore_wait(barrier, jnp.where(first, 24, 26))
+    pl.semaphore_wait(barrier, jnp.where(first, 27, 29))
 
     mine = pl.ds(pl.multiple_of(depth * PIECE, PIECE), PIECE)
 
@@ -175,18 +185,29 @@
 
     totals[...] = jnp.zeros_like(totals)
 
-    def ring_up(slot):
-        return remote(stripes.at[slot], stripes.at[slot], ring_send.at[slot], ring_recv.at[slot], above)
-
-    def ring_down(slot):
-        return remote(stripes.at[slot], stripes.at[slot], ring_send.at[slot], ring_recv.at[slot], below)
-
-    def ring_down_own(slot, other):
-        return remote(stripes.at[slot], stripes.at[slot], ring_send_low.at[other], ring_recv.at[slot], below)
-
-    def forward_step(index, carry):
+    wide = pl.ds(0, WIDE)
+    thin = pl.ds(pl.multiple_of(WIDE + TILE * depth, TILE), TILE)
+
+    def ring_copy(slot, send, device):
+        rows = stripes.at[slot, wide]
+        return remote(rows, rows, send, ring_recv.at[slot], device)
+
+    def thin_copy(slot, send, device):
+        rows = stripes.at[slot, thin]
+        return remote(rows, rows, send, thin_recv.at[slot], device)
+
+    def peer_copy(slot, offset):
+        rows = stripes.at[slot, thin]
+        return remote(rows, rows, peer_send.at[slot, offset], peer_recv.at[slot, depth], peer_devices[offset])
+
+    def peer_arrived(slot, offset):
+        rows = stripes.at[slot, pl.ds(pl.multiple_of(WIDE + TILE * peers[offset], TILE), TILE)]
+        return remote(
+            rows, rows, peer_send.at[slot, offset], peer_recv.at[slot, peers[offset]], peer_devices[offset]
+        )
+
+    def pass_on(index):
         distance, up, other, slot, passes = step_of(index)
-        section = section_of(slot)
 
         @pl.when(index < 2)
         def _():
@@ -201,26 +222,59 @@
                     pl.when(jnp.logical_not(first & (half == other)))(arrived)
                 else:
                     arrived()
-            ring_up(slot).start()
-            ring_down_own(slot, other).start()
+            thin_copy(slot, thin_send.at[slot], above).start()
+            thin_copy(slot, thin_send_low.at[other], below).start()
+            ring_copy(slot, ring_send.at[slot], above).start()
+            ring_copy(slot, ring_send_low.at[other], below).start()
 
         @pl.when(index >= 2)
         def _():
-            ring_up(slot).wait_recv()
+            thin_copy(slot, thin_send.at[slot], above).wait_recv()
 
         @pl.when(passes & (up == 0))
         def _():
-            ring_up(slot).start()
+            thin_copy(slot, thin_send.at[slot], above).start()
 
         @pl.when(passes & (up == 1))
         def _():
-            ring_down(slot).start()
-
-        load_of(section).wait()
-        totals[...] += jnp.dot(blocks[section], stripes[slot], preferred_element_type=jnp.float32)
+            thin_copy(slot, thin_send.at[slot], below).start()
+
+        @pl.when(index >= 2)
+        def _():
+            for offset in range(3):
+                peer_copy(slot, offset).start()
+            ring_copy(slot, ring_send.at[slot], above).wait_recv()
+
+        @pl.when(passes & (up == 0))
+        def _():
+            ring_copy(slot, ring_send.at[slot], above).start()
+
+        @pl.when(passes & (up == 1))
+        def _():
+            ring_copy(slot, ring_send.at[slot], below).start()
+
+    def forward_step(count, carry):
+        @pl.when(count < SECTIONS)
+        def _():
+            pass_on(count)
+
+        @pl.when(count >= LAG)
+        def _():
+            index = count - LAG
+            slot = step_of(index)[3]
+            section = section_of(slot)
+
+            @pl.when(index >= 2)
+            def _():
+                for offset in range(3):
+                    peer_arrived(slot, offset).wait_recv()
+
+            load_of(section).wait()
+            totals[...] += jnp.dot(blocks[section], stripes[slot], preferred_element_type=jnp.float32)
+
         return carry
 
-    lax.fori_loop(0, SECTIONS, forward_step, 0)
+    lax.fori_loop(0, SECTIONS + LAG, forward_step, 0)
 
     def part_copy(offset):
         target = pl.ds(pl.multiple_of(beside[offset][1] * PIECE, PIECE), PIECE)
@@ -269,29 +323,59 @@
             owners[other][piece],
         )
 
-    def back_arrived(slot):
-        return remote(going.at[slot], coming.at[slot], back_send.at[slot], back_recv.at[slot], above)
-
-    def back_arrived_low(slot, other):
-        return remote(going.at[slot], coming_low.at[other], back_send.at[slot], back_recv_low.at[other], below)
-
-    def backward_step(count, carry):
-        index = SECTIONS - 1 - count
+    def back_copy(slot, target, recv, device):
+        return remote(going.at[slot], target, back_send.at[slot], recv, device)
+
+    def back_thin_copy(slot, target, recv, device):
+        return remote(going_thin.at[slot], target, back_thin_send.at[slot], recv, device)
+
+    def give_copy(slot, offset):
+        return remote(
+            given.at[slot, offset], taken.at[slot, depth], give_send.at[slot, offset], give_recv.at[slot, depth],
+            peer_devices[offset],
+        )
+
+    def give_arrived(slot, offset):
+        return remote(
+            given.at[slot, offset], taken.at[slot, peers[offset]], give_send.at[slot, offset],
+            give_recv.at[slot, peers[offset]], peer_devices[offset],
+        )
+
+    def multiply(index, held):
+        slot = step_of(index)[3]
+        sums[held] = jnp.dot(pushed[...], blocks[section_of(slot)], preferred_element_type=jnp.float32)
+
+        @pl.when(index >= 2)
+        def _():
+            for offset in range(3):
+                lanes = pl.ds(pl.multiple_of(WIDE + TILE * peers[offset], TILE), TILE)
+                given[slot, offset] = sums[held, :, lanes].astype(jnp.bfloat16)
+                give_copy(slot, offset).start()
+
+    def reduce(index, held):
         distance, up, other, slot, passes = step_of(index)
-        section = section_of(slot)
-        sums[...] = jnp.dot(pushed[...], blocks[section], preferred_element_type=jnp.float32)
+
+        @pl.when(index >= 2)
+        def _():
+            for offset in range(3):
+                give_arrived(slot, offset).wait_recv()
+                sums[held, :, thin] += taken[slot, peers[offset]].astype(jnp.float32)
 
         @pl.when(passes | (index < 2))
         def _():
-            back_arrived(slot).wait_recv()
-            sums[...] += coming[slot].astype(jnp.float32)
+            back_thin_copy(slot, coming_thin.at[slot], back_thin_recv.at[slot], above).wait_recv()
+            sums[held, :, thin] += coming_thin[slot].astype(jnp.float32)
+            back_copy(slot, coming.at[slot], back_recv.at[slot], above).wait_recv()
+            sums[held, :, wide] += coming[slot].astype(jnp.float32)
 
         @pl.when(index < 2)
         def _():
-            back_arrived_low(slot, other).wait_recv()
-            sums[...] += coming_low[other].astype(jnp.float32)
+            back_thin_copy(slot, coming_thin_low.at[other], back_thin_recv_low.at[other], below).wait_recv()
+            sums[held, :, thin] += coming_thin_low[other].astype(jnp.float32)
+            back_copy(slot, coming_low.at[other], back_recv_low.at[other], below).wait_recv()
+            sums[held, :, wide] += coming_low[other].astype(jnp.float32)
             for piece in range(4):
-                shares[other, piece] = sums[:, piece * PIECE:(piece + 1) * PIECE].astype(jnp.bfloat16)
+                shares[other, piece] = sums[held, :, pl.ds(piece * PIECE, PIECE)].astype(jnp.bfloat16)
 
         for which in range(2):
             @pl.when((index < 2) & (other == which))
@@ -310,21 +394,34 @@
 
         @pl.when(index >= 2)
         def _():
-            going[slot] = sums[...].astype(jnp.bfloat16)
+            going_thin[slot] = sums[held, :, thin].astype(jnp.bfloat16)
+            going[slot] = sums[held, :, wide].astype(jnp.bfloat16)
 
         last_far = distance == 4
 
         @pl.when((index >= 2) & (((up == 0) & jnp.logical_not(last_far)) | (last_far & (other == 0))))
         def _():
-            remote(going.at[slot], coming.at[slot], back_send.at[slot], back_recv.at[slot], below).start()
+            back_thin_copy(slot, coming_thin.at[slot], back_thin_recv.at[slot], below).start()
+            back_copy(slot, coming.at[slot], back_recv.at[slot], below).start()
 
         @pl.when((index >= 2) & (((up == 1) & (distance > 1)) | (last_far & (other == 1))))
         def _():
-            remote(going.at[slot], coming.at[slot], back_send.at[slot], back_recv.at[slot], above).start()
+            back_thin_copy(slot, coming_thin.at[slot], back_thin_recv.at[slot], above).start()
+            back_copy(slot, coming.at[slot], back_recv.at[slot], above).start()
 
         @pl.when((index >= 2) & (up == 1) & (distance == 1))
         def _():
-            remote(going.at[slot], coming_low.at[other], back_send.at[slot], back_recv_low.at[other], above).start()
+            back_thin_copy(slot, coming_thin_low.at[other], back_thin_recv_low.at[other], above).start()
+            back_copy(slot, coming_low.at[other], back_recv_low.at[other], above).start()
+
+    def backward_step(count, carry):
+        @pl.when(count < SECTIONS)
+        def _():
+            multiply(SECTIONS - 1 - count, count % (LAG + 1))
+
+        @pl.when(count >= LAG)
+        def _():
+            reduce(SECTIONS - 1 - (count - LAG), (count - LAG) % (LAG + 1))
 
         for step in range(1, 8):
             @pl.when(count == 2 * step)
@@ -335,7 +432,7 @@
 
         return carry
 
-    lax.fori_loop(0, SECTIONS, backward_step, 0)
+    lax.fori_loop(0, SECTIONS + LAG, backward_step, 0)
 
     term_copy(7).wait_recv()
     weight_grad[...] = terms[7] + other_terms[7]
@@ -380,19 +477,42 @@
 
         @pl.when(index < 2)
         def _():
-            ring_down_own(slot, other).wait_send()
+            ring_copy(slot, ring_send_low.at[other], below).wait_send()
+            thin_copy(slot, thin_send_low.at[other], below).wait_send()
 
         @pl.when(passes | (index < 2))
         def _():
-            ring_up(slot).wait_send()
+            ring_copy(slot, ring_send.at[slot], above).wait_send()
+            thin_copy(slot, thin_send.at[slot], above).wait_send()
 
         @pl.when(index >= 2)
         def _():
-            back_arrived(slot).wait_send()
+            back_copy(slot, coming.at[slot], back_recv.at[slot], above).wait_send()
+            back_thin_copy(slot, coming_thin.at[slot], back_thin_recv.at[slot], above).wait_send()
+            for offset in range(3):
+                peer_copy(slot, offset).wait_send()
+                give_copy(slot, offset).wait_send()
 
         return carry
 
     lax.fori_loop(0, SECTIONS, sent_step, 0)
+
+
+def finish_kernel(act, feature_grad, weight_grad, act_out, feature_out, weight_out):
+    act_out[...] = act[...]
+    feature_out[...] = feature_grad[...]
+    weight_out[...] = weight_grad[...]
+
+
+def finish(*results):
+    vmem = pl.BlockSpec(memory_space=pltpu.VMEM)
+    return pl.pallas_call(
+        finish_kernel,
+        out_shape=tuple(jax.ShapeDtypeStruct(value.shape, value.dtype) for value in results),
+        in_specs=[vmem] * 3,
+        out_specs=(vmem,) * 3,
+        cost_estimate=pl.CostEstimate(flops=0, bytes_accessed=640_000, transcendentals=0),
+    )(*results)
 
 
 def layer(features, norm_row, weight, cotangent, dense):
@@ -416,17 +536,25 @@
             pltpu.VMEM((3, PIECE, FEAT), f32),
             pltpu.VMEM((FEAT, STRIPE), bf16),
             pltpu.VMEM((FEAT, PIECE), bf16),
-            pltpu.VMEM((FEAT, STRIPE), f32),
-            pltpu.VMEM((SECTIONS, FEAT, STRIPE), bf16),
-            pltpu.VMEM((SECTIONS, FEAT, STRIPE), bf16),
-            pltpu.VMEM((2, FEAT, STRIPE), bf16),
+            pltpu.VMEM((LAG + 1, FEAT, STRIPE), f32),
+            pltpu.VMEM((SECTIONS, FEAT, WIDE), bf16),
+            pltpu.VMEM((SECTIONS, FEAT, TILE), bf16),
+            pltpu.VMEM((SECTIONS, FEAT, WIDE), bf16),
+            pltpu.VMEM((SECTIONS, FEAT, TILE), bf16),
+            pltpu.VMEM((2, FEAT, WIDE), bf16),
+            pltpu.VMEM((2, FEAT, TILE), bf16),
+            pltpu.VMEM((SECTIONS, 3, FEAT, TILE), bf16),
+            pltpu.VMEM((SECTIONS, 4, FEAT, TILE), bf16),
             pltpu.VMEM((2, 4, FEAT, PIECE), bf16),
             pltpu.VMEM((2, 4, FEAT, PIECE), bf16),
             pltpu.VMEM((8, FEAT, FEAT), f32),
             pltpu.VMEM((8, FEAT, FEAT), f32),
             dma((SECTIONS,)), dma((2, 4)), dma((2, 4)), dma((SECTIONS,)), dma((2,)), dma((SECTIONS,)),
+            dma((SECTIONS,)), dma((2,)), dma((SECTIONS,)), dma((SECTIONS, 3)), dma((SECTIONS, 4)),
             dma((3,)), dma((3,)), dma((3,)), dma((3,)),
-            dma((SECTIONS,)), dma((SECTIONS,)), dma((2,)), dma((2, 4)), dma((2, 4)), dma((8,)), dma((8,)),
+            dma((SECTIONS,)), dma((SECTIONS,)), dma((2,)), dma((SECTIONS,)), dma((SECTIONS,)), dma((2,)),
+            dma((SECTIONS, 3)), dma((SECTIONS, 4)),
+            dma((2, 4)), dma((2, 4)), dma((8,)), dma((8,)),
         ],
         compiler_params=pltpu.CompilerParams(
             collective_id=0, has_side_effects=True, vmem_limit_bytes=60 * 1024 * 1024
@@ -437,7 +565,7 @@
 
 def per_device(features, norm_scale, weight, cotangent, tile_rows, tile_cols, tile_masks, tile_counts):
     dense = dense_blocks(tile_rows[0, 0], tile_cols[0, 0], tile_counts[0, 0], tile_masks[0, 0])
-    return layer(features, norm_scale.reshape(1, -1), weight, cotangent, dense)
+    return finish(*layer(features, norm_scale.reshape(1, -1), weight, cotangent, dense))
 
 
 def solution(mesh):

time: 176 us -> 156 us (0.89)
  Pallas kernels: 165 us -> 155 us
  local copies, waits for them, and re-layouts: 9.43 us -> 0 us
    pallas_call x1, Pallas kernels: 142 us -> 132 us  [layer(): pl.pallas_call(layer_kernel, out_shape=(jax.ShapeDtypeStruct((PIECE, FEAT...]
    unnamed x11 -> x0, local copies, waits for them, and re-layouts: 9.43 us -> none
where the time goes in v2:
time: 156 us
  Pallas kernels  155 us (99%)
    pallas_call x1, Pallas kernels, layer(): pl.pallas_call(layer_kernel, out_shape=(jax.ShapeDtypeStruct((PIECE, FEAT...  132 us
    pallas_call x1, Pallas kernels, dense_blocks(): pl.pallas_call(dense_kernel, out_shape=jax.ShapeDtypeStruct((SECTIONS, ST...  21.7 us

profile of v2, /device:TPU:1, one launch (start us, length us, event | category | flops | bytes accessed | tf_op | source)
XLA Modules:
  0.0 155.9 jit_solution(6418074223485205162)
XLA Ops:
  0.6 21.7 %shard_map.103.dense = bf16[16,1024,1024]{2,1,0:T(8,128)(2,1)} custom-call(s32[16,48]{1,0:T(8,128)} %bitcast.6, s32[16,48]{1,0:T(8,128)} %bitcast.7, s32[16]{0:T(128)} %bitcast.9, s32[16,48,2048]{2,1,0:T(8,128)} %bitcast.5), custom_call_target="tpu_custom_call" | custom-call | flops 50000000 | bytes 40000000 | tf_op jit(solution)/shard_map/pallas_call | solution.py:66
  22.3 131.8 %shard_map.104 = (f32[256,128]{1,0:T(8,128)}, f32[256,128]{1,0:T(8,128)}, f32[128,128]{1,0:T(8,128)}) custom-call(f32[256,128]{1,0:T(8,128)} %features.1, f32[1,256]{1,0:T(1,128)} %bitcast.8, bf16[128,128]{1,0:T(8,128)(2,1)} %weight.1, f32[256,128]{1,0:T(8,128)} %cotangent.1, bf16[16,1024,1024]{2,1,0:T(8,128)(2,1)} %shard_map.103.dense), custom_call_target="tpu_custom_call" | custom-call | flops 8999999488 | bytes 34000000 | tf_op jit(solution)/shard_map/pallas_call | solution.py:522
  154.2 1.7 %shard_map.105 = (f32[256,128]{1,0:T(8,128)}, f32[256,128]{1,0:T(8,128)}, f32[128,128]{1,0:T(8,128)}) custom-call(f32[256,128]{1,0:T(8,128)} %get-tuple-element.6.act, f32[256,128]{1,0:T(8,128)} %get-tuple-element.7.feature_grad, f32[128,128]{1,0:T(8,128)} %get-tuple-element.8.weight_grad), custom_call_target="tpu_custom_call" | custom-call | bytes 640000 | tf_op jit(solution)/shard_map/pallas_call | solution.py:509

commit v3 on v2

--- a/solution.py
+++ b/solution.py
@@ -14,52 +14,56 @@
 RING = 8
 UNROLL = 4
 WIDE = 512
-LAG = 2
+LAG = 3
+PAIR = 2
 MESH = pl.DeviceIdType.MESH
 
 
 def dense_kernel(rows, cols, counts, words, out, packed):
-    section = pl.program_id(0)
-    live_count = counts[section]
-    out[...] = jnp.zeros_like(out)
-    packed[pl.ds(CAP, UNROLL)] = jnp.zeros((UNROLL, 4, 128), jnp.int32)
-    for eight in range(CAP // 8):
-        slots = pl.ds(eight * 8, 8)
-        for part in range(4):
-            value = words[0, slots, pl.ds(part * 512, 128)]
-            for step in range(1, 4):
-                value = value | (words[0, slots, pl.ds(part * 512 + step * 128, 128)] << (8 * step))
-            packed[slots, part, :] = value
     lane = lax.broadcasted_iota(jnp.int32, (8, 128), 1)
     row = lax.broadcasted_iota(jnp.int32, (8, 128), 0)
     place = row * 16 + lax.rem(lane, 16)
     bit = lax.div(lane, 16)
-
-    def near_of(group):
-        return [
-            jnp.take_along_axis(
-                jnp.broadcast_to(packed[group * UNROLL + index, pl.ds(part, 1), :], (8, 128)),
-                place, axis=1, mode="promise_in_bounds",
-            )
-            for index in range(UNROLL) for part in range(4)
-        ]
-
-    def group_step(group, nears):
-        later = near_of(group + 1)
-        for index in range(UNROLL):
-            slot = group * UNROLL + index
-            live = jnp.where(slot < live_count, 1, 0)
-            strips = [
-                ((nears[4 * index + part] >> (bit + 8 * step)) & live).astype(jnp.float32)
-                for part in range(4) for step in range(4)
+    out[...] = jnp.zeros_like(out)
+    for which in range(PAIR):
+        packed[which, pl.ds(CAP, UNROLL)] = jnp.zeros((UNROLL, 4, 128), jnp.int32)
+        for eight in range(CAP // 8):
+            slots = pl.ds(eight * 8, 8)
+            for part in range(4):
+                value = words[which, slots, pl.ds(part * 512, 128)]
+                for step in range(1, 4):
+                    value = value | (words[which, slots, pl.ds(part * 512 + step * 128, 128)] << (8 * step))
+                packed[which, slots, part, :] = value
+
+    for which in range(PAIR):
+        section = pl.program_id(0) * PAIR + which
+        live_count = counts[section]
+
+        def near_of(group, which=which):
+            return [
+                jnp.take_along_axis(
+                    jnp.broadcast_to(packed[which, group * UNROLL + index, pl.ds(part, 1), :], (8, 128)),
+                    place, axis=1, mode="promise_in_bounds",
+                )
+                for index in range(UNROLL) for part in range(4)
             ]
-            tile = jnp.concatenate(strips, axis=0).astype(jnp.bfloat16)
-            top = pl.multiple_of(rows[section, slot] * TILE, TILE)
-            left = pl.multiple_of(cols[section, slot] * TILE, TILE)
-            out[0, pl.ds(top, TILE), pl.ds(left, TILE)] += tile
-        return later
-
-    lax.fori_loop(0, (live_count + UNROLL - 1) // UNROLL, group_step, near_of(0))
+
+        def group_step(group, nears, which=which, section=section, live_count=live_count, near_of=near_of):
+            later = near_of(group + 1)
+            for index in range(UNROLL):
+                slot = group * UNROLL + index
+                live = jnp.where(slot < live_count, 1, 0)
+                strips = [
+                    ((nears[4 * index + part] >> (bit + 8 * step)) & live).astype(jnp.float32)
+                    for part in range(4) for step in range(4)
+                ]
+                tile = jnp.concatenate(strips, axis=0).astype(jnp.bfloat16)
+                top = pl.multiple_of(rows[section, slot] * TILE, TILE)
+                left = pl.multiple_of(cols[section, slot] * TILE, TILE)
+                out[which, pl.ds(top, TILE), pl.ds(left, TILE)] += tile
+            return later
+
+        lax.fori_loop(0, (live_count + UNROLL - 1) // UNROLL, group_step, near_of(0))
 
 
 def dense_blocks(tile_rows, tile_cols, tile_counts, tile_masks):
@@ -68,10 +72,10 @@
         out_shape=jax.ShapeDtypeStruct((SECTIONS, STRIPE, STRIPE), jnp.bfloat16),
         grid_spec=pltpu.PrefetchScalarGridSpec(
             num_scalar_prefetch=3,
-            grid=(SECTIONS,),
-            in_specs=[pl.BlockSpec((1, CAP, 2048), lambda k, *_: (k, 0, 0))],
-            out_specs=pl.BlockSpec((1, STRIPE, STRIPE), lambda k, *_: (k, 0, 0)),
-            scratch_shapes=[pltpu.VMEM((CAP + UNROLL, 4, 128), jnp.int32)],
+            grid=(SECTIONS // PAIR,),
+            in_specs=[pl.BlockSpec((PAIR, CAP, 2048), lambda k, *_: (k, 0, 0))],
+            out_specs=pl.BlockSpec((PAIR, STRIPE, STRIPE), lambda k, *_: (k, 0, 0)),
+            scratch_shapes=[pltpu.VMEM((PAIR, CAP + UNROLL, 4, 128), jnp.int32)],
         ),
         compiler_params=pltpu.CompilerParams(vmem_limit_bytes=60 * 1024 * 1024),
         cost_estimate=pl.CostEstimate(flops=50_000_000, bytes_accessed=40_000_000, transcendentals=0),
@@ -80,9 +84,9 @@
 
 def layer_kernel(
     features, norm, weight, cotangent, dense, act, feature_grad, weight_grad,
-    blocks, stripes, own, totals, parts, pushed, own_pushed, sums, going, going_thin, coming, coming_thin, coming_low,
+    blocks, stripes, own, mate, mate_out, mate_in, totals, parting, parts, pushed, own_pushed, sums, going, going_thin, coming, coming_thin, coming_low,
     coming_thin_low, given, taken, shares, shared, terms, other_terms,
-    dense_sem, team_send, team_recv, ring_send, ring_send_low, ring_recv, thin_send, thin_send_low, thin_recv, peer_send,
+    dense_sem, mate_send, mate_recv, mate_back_send, mate_back_recv, team_send, team_recv, ring_send, ring_send_low, ring_recv, thin_send, thin_send_low, thin_recv, peer_send,
     peer_recv, part_send, part_recv, push_send, push_recv, back_send, back_recv, back_recv_low, back_thin_send,
     back_thin_recv, back_thin_recv_low, give_send, give_recv, share_send, share_recv, term_send, term_recv,
 ):
@@ -105,11 +109,19 @@
 
     above = (((z + 1) % RING) * 8 + loop % 8, depth)
     below = (((z + RING - 1) % RING) * 8 + loop % 8, depth)
-    team = [[((z * 2 + other) * 4 + (y + member) % 4, member) for member in range(4)] for other in range(2)]
-    owners = [[((z * 2 + other) * 4 + kind, piece) for piece in range(4)] for other in range(2)]
+    mate_node = z * 2 + 1 - half
+    mate_device = (mate_node * 4 + y, depth)
+    team = [(node * 4 + (y + member) % 4, member) for member in range(4)]
+    owners = [(node * 4 + kind, piece) for piece in range(4)]
     beside = [(loop, (depth + offset) % 4) for offset in range(1, 4)]
-    peers = [(depth + offset) % 4 for offset in range(1, 4)]
-    peer_devices = [(node * 4 + (kind + member) % 4, member) for member in peers]
+    two = (depth + 2) % 4
+
+    def peer_device(member):
+        return (node * 4 + (kind + member) % 4, member)
+
+    def around(other):
+        return (depth + 3 + 2 * other) % 4, (depth + 1 + 2 * other) % 4
+
     before = [(depth + 4 - offset) % 4 for offset in range(1, 4)]
     partners = [
         (loop, toggled(depth, 1)), (loop, toggled(depth, 2)), (toggled(loop, 4), depth), (toggled(loop, 1), depth),
@@ -123,7 +135,7 @@
         distance = (index + 2) // 4
         up = ((index + 2) // 2) % 2
         other = index % 2
-        slot = ((z + RING - distance + 2 * distance * up) % RING) * 2 + other
+        slot = ((z + RING - distance + 2 * distance * up) % RING) * 2 + (half + other) % 2
         passes = (index >= 2) & ((distance < 3) | ((distance == 3) & (other == up)))
         return distance, up, other, slot, passes
 
@@ -137,18 +149,17 @@
     lax.fori_loop(0, SECTIONS, load_step, 0)
 
     barrier = pltpu.get_barrier_semaphore()
-    for device in [above, below] + beside + peer_devices + [partners[2], partners[3], partners[4], partners[6], partners[7]]:
+    for device in [above, below] + beside + [peer_device((depth + offset) % 4) for offset in range(1, 4)] + [mate_device, partners[3], partners[4], partners[6], partners[7]]:
         pl.semaphore_signal(barrier, inc=1, device_id=device, device_id_type=MESH)
-    for other in range(2):
-        for index in range(4):
-            def greet(other=other, index=index):
-                pl.semaphore_signal(barrier, inc=1, device_id=team[other][index], device_id_type=MESH)
-                pl.semaphore_signal(barrier, inc=1, device_id=owners[other][index], device_id_type=MESH)
-
-            if index == 0:
-                pl.when(jnp.logical_not(first & (half == other)))(greet)
-            else:
-                greet()
+    for index in range(4):
+        def greet(index=index):
+            pl.semaphore_signal(barrier, inc=1, device_id=team[index], device_id_type=MESH)
+            pl.semaphore_signal(barrier, inc=1, device_id=owners[index], device_id_type=MESH)
+
+        if index == 0:
+            pl.when(jnp.logical_not(first))(greet)
+        else:
+            greet()
 
     order_row = lax.broadcasted_iota(jnp.int32, (TILE, TILE), 0)
     order_col = lax.broadcasted_iota(jnp.int32, (TILE, TILE), 1)
@@ -161,19 +172,24 @@
             order.astype(jnp.bfloat16), scaled[tile * TILE:(tile + 1) * TILE], preferred_element_type=jnp.float32
         ).astype(jnp.bfloat16)
 
-    pl.semaphore_wait(barrier, jnp.where(first, 27, 29))
+    pl.semaphore_wait(barrier, jnp.where(first, 19, 21))
 
     mine = pl.ds(pl.multiple_of(depth * PIECE, PIECE), PIECE)
 
     def team_copy(other, member):
         return remote(
-            own, stripes.at[node, mine], team_send.at[other, member], team_recv.at[half, depth], team[other][member]
+            own if other == 0 else mate, stripes.at[node if other == 0 else mate_node, mine],
+            team_send.at[other, member], team_recv.at[other, depth], team[member],
         )
 
+    mate_copy = remote(own, mate, mate_send, mate_recv, mate_device)
+    mate_copy.start()
     for other in range(2):
+        if other == 1:
+            mate_copy.wait_recv()
         for member in range(4):
             if member == 0:
-                @pl.when(jnp.logical_not(first & (half == other)))
+                @pl.when(jnp.logical_not(first))
                 def _(other=other):
                     team_copy(other, 0).start()
             else:
@@ -182,6 +198,7 @@
     @pl.when(first)
     def _():
         stripes[node, 0:PIECE, :] = own[...]
+        stripes[mate_node, 0:PIECE, :] = mate[...]
 
     totals[...] = jnp.zeros_like(totals)
 
@@ -196,15 +213,12 @@
         rows = stripes.at[slot, thin]
         return remote(rows, rows, send, thin_recv.at[slot], device)
 
-    def peer_copy(slot, offset):
-        rows = stripes.at[slot, thin]
-        return remote(rows, rows, peer_send.at[slot, offset], peer_recv.at[slot, depth], peer_devices[offset])
-
-    def peer_arrived(slot, offset):
-        rows = stripes.at[slot, pl.ds(pl.multiple_of(WIDE + TILE * peers[offset], TILE), TILE)]
-        return remote(
-            rows, rows, peer_send.at[slot, offset], peer_recv.at[slot, peers[offset]], peer_devices[offset]
-        )
+    def quarter(slot, member):
+        return stripes.at[slot, pl.ds(pl.multiple_of(WIDE + TILE * member, TILE), TILE)]
+
+    def peer_copy(slot, member, which, target):
+        rows = quarter(slot, member)
+        return remote(rows, rows, peer_send.at[slot, which], peer_recv.at[slot, member], peer_device(target))
 
     def pass_on(index):
         distance, up, other, slot, passes = step_of(index)
@@ -219,7 +233,7 @@
                     ).wait_recv()
 
                 if piece == 0:
-                    pl.when(jnp.logical_not(first & (half == other)))(arrived)
+                    pl.when(jnp.logical_not(first))(arrived)
                 else:
                     arrived()
             thin_copy(slot, thin_send.at[slot], above).start()
@@ -241,8 +255,9 @@
 
         @pl.when(index >= 2)
         def _():
-            for offset in range(3):
-                peer_copy(slot, offset).start()
+            near, far = around(other)
+            peer_copy(slot, depth, 0, far).start()
+            peer_copy(slot, depth, 1, near).start()
             ring_copy(slot, ring_send.at[slot], above).wait_recv()
 
         @pl.when(passes & (up == 0))
@@ -258,16 +273,25 @@
         def _():
             pass_on(count)
 
+        @pl.when((count >= 3) & (count < SECTIONS + 1))
+        def _():
+            distance, up, other, slot, passes = step_of(count - 1)
+            near, far = around(other)
+            relay = peer_copy(slot, near, 2, far)
+            relay.wait_recv()
+            relay.start()
+
         @pl.when(count >= LAG)
         def _():
             index = count - LAG
-            slot = step_of(index)[3]
+            distance, up, other, slot, passes = step_of(index)
             section = section_of(slot)
 
             @pl.when(index >= 2)
             def _():
-                for offset in range(3):
-                    peer_arrived(slot, offset).wait_recv()
+                near, far = around(other)
+                peer_copy(slot, far, 0, near).wait_recv()
+                peer_copy(slot, two, 0, near).wait_recv()
 
             load_of(section).wait()
             totals[...] += jnp.dot(blocks[section], stripes[slot], preferred_element_type=jnp.float32)
@@ -276,18 +300,26 @@
 
     lax.fori_loop(0, SECTIONS + LAG, forward_step, 0)
 
-    def part_copy(offset):
-        target = pl.ds(pl.multiple_of(beside[offset][1] * PIECE, PIECE), PIECE)
+    twin, cross = toggled(depth, 1), toggled(depth, 2)
+
+    def piece_of(member):
+        return pl.ds(pl.multiple_of(member * PIECE, PIECE), PIECE)
+
+    def part_copy(which):
+        source = parting if which == 2 else totals.at[piece_of(toggled(twin, 2) if which == 1 else twin)]
         return remote(
-            totals.at[target], parts.at[offset], part_send.at[offset], part_recv.at[offset], beside[offset]
+            source, parts.at[which], part_send.at[which], part_recv.at[which], (loop, cross if which == 2 else twin)
         )
 
-    for offset in range(3):
-        part_copy(offset).start()
-    summed = totals[mine, :]
-    for offset in range(3):
-        part_copy(offset).wait_recv()
-        summed = summed + parts[offset]
+    part_copy(1).start()
+    part_copy(0).start()
+    part_copy(1).wait_recv()
+    parting[...] = totals[piece_of(cross), :] + parts[1]
+    part_copy(2).start()
+    part_copy(0).wait_recv()
+    summed = totals[mine, :] + parts[0]
+    part_copy(2).wait_recv()
+    summed = summed + parts[2]
 
     aggregated_b = (norm_full * summed).astype(jnp.bfloat16)
     pre = jnp.dot(aggregated_b, weight[...], preferred_element_type=jnp.float32)
@@ -319,8 +351,8 @@
 
     def share_copy(other, piece):
         return remote(
-            shares.at[other, piece], shared.at[half, depth], share_send.at[other, piece], share_recv.at[half, depth],
-            owners[other][piece],
+            shares.at[other, piece], shared.at[other, depth], share_send.at[other, piece], share_recv.at[other, depth],
+            owners[piece],
         )
 
     def back_copy(slot, target, recv, device):
@@ -329,37 +361,43 @@
     def back_thin_copy(slot, target, recv, device):
         return remote(going_thin.at[slot], target, back_thin_send.at[slot], recv, device)
 
-    def give_copy(slot, offset):
+    def give_copy(slot, which, target):
         return remote(
-            given.at[slot, offset], taken.at[slot, depth], give_send.at[slot, offset], give_recv.at[slot, depth],
-            peer_devices[offset],
+            given.at[slot, which], taken.at[slot, which], give_send.at[slot, which], give_recv.at[slot, which],
+            peer_device(target),
         )
 
-    def give_arrived(slot, offset):
-        return remote(
-            given.at[slot, offset], taken.at[slot, peers[offset]], give_send.at[slot, offset],
-            give_recv.at[slot, peers[offset]], peer_devices[offset],
-        )
+    def lanes_of(member):
+        return pl.ds(pl.multiple_of(WIDE + TILE * member, TILE), TILE)
 
     def multiply(index, held):
-        slot = step_of(index)[3]
+        distance, up, other, slot, passes = step_of(index)
         sums[held] = jnp.dot(pushed[...], blocks[section_of(slot)], preferred_element_type=jnp.float32)
 
         @pl.when(index >= 2)
         def _():
-            for offset in range(3):
-                lanes = pl.ds(pl.multiple_of(WIDE + TILE * peers[offset], TILE), TILE)
-                given[slot, offset] = sums[held, :, lanes].astype(jnp.bfloat16)
-                give_copy(slot, offset).start()
+            near, far = around(other)
+            given[slot, 0] = sums[held, :, lanes_of(two)].astype(jnp.bfloat16)
+            give_copy(slot, 0, near).start()
+            given[slot, 2] = sums[held, :, lanes_of(far)].astype(jnp.bfloat16)
+            give_copy(slot, 2, far).start()
+
+    def hand_on(index, held):
+        distance, up, other, slot, passes = step_of(index)
+        near, far = around(other)
+        give_copy(slot, 0, near).wait_recv()
+        given[slot, 1] = (sums[held, :, lanes_of(near)] + taken[slot, 0].astype(jnp.float32)).astype(jnp.bfloat16)
+        give_copy(slot, 1, near).start()
 
     def reduce(index, held):
         distance, up, other, slot, passes = step_of(index)
 
         @pl.when(index >= 2)
         def _():
-            for offset in range(3):
-                give_arrived(slot, offset).wait_recv()
-                sums[held, :, thin] += taken[slot, peers[offset]].astype(jnp.float32)
+            near, far = around(other)
+            for which in (1, 2):
+                give_copy(slot, which, near).wait_recv()
+                sums[held, :, thin] += taken[slot, which].astype(jnp.float32)
 
         @pl.when(passes | (index < 2))
         def _():
@@ -376,21 +414,16 @@
             sums[held, :, wide] += coming_low[other].astype(jnp.float32)
             for piece in range(4):
                 shares[other, piece] = sums[held, :, pl.ds(piece * PIECE, PIECE)].astype(jnp.bfloat16)
-
-        for which in range(2):
-            @pl.when((index < 2) & (other == which))
-            def _(which=which):
-                for piece in range(4):
-                    if piece == 0:
-                        @pl.when(jnp.logical_not(first & (half == which)))
-                        def _():
-                            share_copy(which, 0).start()
-
-                        @pl.when(first & (half == which))
-                        def _():
-                            shared[half, 0] = shares[which, 0]
-                    else:
-                        share_copy(which, piece).start()
+                if piece == 0:
+                    @pl.when(jnp.logical_not(first))
+                    def _():
+                        share_copy(other, 0).start()
+
+                    @pl.when(first)
+                    def _():
+                        shared[other, 0] = shares[other, 0]
+                else:
+                    share_copy(other, piece).start()
 
         @pl.when(index >= 2)
         def _():
@@ -418,6 +451,10 @@
         @pl.when(count < SECTIONS)
         def _():
             multiply(SECTIONS - 1 - count, count % (LAG + 1))
+
+        @pl.when((count >= 1) & (count < SECTIONS - 1))
+        def _():
+            hand_on(SECTIONS - count, (count - 1) % (LAG + 1))
 
         @pl.when(count >= LAG)
         def _():
@@ -434,28 +471,38 @@
 
     lax.fori_loop(0, SECTIONS + LAG, backward_step, 0)
 
-    term_copy(7).wait_recv()
-    weight_grad[...] = terms[7] + other_terms[7]
-
-    gathered = jnp.zeros((FEAT, PIECE), jnp.float32)
-    for other in range(2):
+    def shared_sum(other):
+        gathered = jnp.zeros((FEAT, PIECE), jnp.float32)
         for member in range(4):
-            def share_arrived(other=other, member=member):
+            def share_arrived(member=member):
                 remote(
                     shares.at[0, 0], shared.at[other, member], share_send.at[0, 0], share_recv.at[other, member], above
                 ).wait_recv()
 
             if member == 0:
-                pl.when(jnp.logical_not(first & (half == other)))(share_arrived)
+                pl.when(jnp.logical_not(first))(share_arrived)
             else:
                 share_arrived()
             gathered = gathered + shared[other, member].astype(jnp.float32)
+        return gathered
+
+    mate_out[...] = shared_sum(1).astype(jnp.bfloat16)
+    mate_back = remote(mate_out, mate_in, mate_back_send, mate_back_recv, mate_device)
+    mate_back.start()
+    gathered = shared_sum(0)
+    mate_back.wait_recv()
+    gathered = gathered + mate_in[...].astype(jnp.float32)
     for tile in range(2):
         feature_grad[pl.ds(tile * TILE, TILE), :] = norm_full[tile * TILE:(tile + 1) * TILE] * lax.dot_general(
             order, gathered[:, tile * TILE:(tile + 1) * TILE], (((0,), (1,)), ((), ())),
             precision=lax.Precision.HIGHEST, preferred_element_type=jnp.float32,
         )
 
+    term_copy(7).wait_recv()
+    weight_grad[...] = terms[7] + other_terms[7]
+
+    mate_copy.wait_send()
+    mate_back.wait_send()
     for other in range(2):
         for index in range(4):
             def sent(other=other, index=index):
@@ -463,7 +510,7 @@
                 share_copy(other, index).wait_send()
 
             if index == 0:
-                pl.when(jnp.logical_not(first & (half == other)))(sent)
+                pl.when(jnp.logical_not(first))(sent)
             else:
                 sent()
     for offset in range(3):
@@ -489,9 +536,9 @@
         def _():
             back_copy(slot, coming.at[slot], back_recv.at[slot], above).wait_send()
             back_thin_copy(slot, coming_thin.at[slot], back_thin_recv.at[slot], above).wait_send()
-            for offset in range(3):
-                peer_copy(slot, offset).wait_send()
-                give_copy(slot, offset).wait_send()
+            for which in range(3):
+                peer_copy(slot, depth, which, two).wait_send()
+                give_copy(slot, which, two).wait_send()
 
         return carry
 
@@ -532,7 +579,11 @@
             pltpu.VMEM((SECTIONS, STRIPE, STRIPE), bf16),
             pltpu.VMEM((SECTIONS, STRIPE, FEAT), bf16),
             pltpu.VMEM((PIECE, FEAT), bf16),
+            pltpu.VMEM((PIECE, FEAT), bf16),
+            pltpu.VMEM((FEAT, PIECE), bf16),
+            pltpu.VMEM((FEAT, PIECE), bf16),
             pltpu.VMEM((STRIPE, FEAT), f32),
+            pltpu.VMEM((PIECE, FEAT), f32),
             pltpu.VMEM((3, PIECE, FEAT), f32),
             pltpu.VMEM((FEAT, STRIPE), bf16),
             pltpu.VMEM((FEAT, PIECE), bf16),
@@ -544,16 +595,17 @@
             pltpu.VMEM((2, FEAT, WIDE), bf16),
             pltpu.VMEM((2, FEAT, TILE), bf16),
             pltpu.VMEM((SECTIONS, 3, FEAT, TILE), bf16),
-            pltpu.VMEM((SECTIONS, 4, FEAT, TILE), bf16),
+            pltpu.VMEM((SECTIONS, 3, FEAT, TILE), bf16),
             pltpu.VMEM((2, 4, FEAT, PIECE), bf16),
             pltpu.VMEM((2, 4, FEAT, PIECE), bf16),
             pltpu.VMEM((8, FEAT, FEAT), f32),
             pltpu.VMEM((8, FEAT, FEAT), f32),
-            dma((SECTIONS,)), dma((2, 4)), dma((2, 4)), dma((SECTIONS,)), dma((2,)), dma((SECTIONS,)),
+            dma((SECTIONS,)), dma, dma, dma, dma,
+            dma((2, 4)), dma((2, 4)), dma((SECTIONS,)), dma((2,)), dma((SECTIONS,)),
             dma((SECTIONS,)), dma((2,)), dma((SECTIONS,)), dma((SECTIONS, 3)), dma((SECTIONS, 4)),
             dma((3,)), dma((3,)), dma((3,)), dma((3,)),
             dma((SECTIONS,)), dma((SECTIONS,)), dma((2,)), dma((SECTIONS,)), dma((SECTIONS,)), dma((2,)),
-            dma((SECTIONS, 3)), dma((SECTIONS, 4)),
+            dma((SECTIONS, 3)), dma((SECTIONS, 3)),
             dma((2, 4)), dma((2, 4)), dma((8,)), dma((8,)),
         ],
         compiler_params=pltpu.CompilerParams(

time: 156 us -> 154 us (0.987)
  Pallas kernels: 155 us -> 153 us
    pallas_call x1, Pallas kernels: 21.7 us -> 18.7 us  [dense_blocks(): pl.pallas_call(dense_kernel, out_shape=jax.ShapeDtypeStruct((SECTIONS, ST...]
where the time goes in v3:
time: 154 us
  Pallas kernels  153 us (99%)
    pallas_call x1, Pallas kernels, layer(): pl.pallas_call(layer_kernel, out_shape=(jax.ShapeDtypeStruct((PIECE, FEAT...  133 us
    pallas_call x1, Pallas kernels, dense_blocks(): pl.pallas_call(dense_kernel, out_shape=jax.ShapeDtypeStruct((SECTIONS, ST...  18.7 us

profile of v3, /device:TPU:1, one launch (start us, length us, event | category | flops | bytes accessed | tf_op | source)
XLA Modules:
  0.0 153.8 jit_solution(17274329509088592298)
XLA Ops:
  0.6 18.7 %shard_map.103.dense = bf16[16,1024,1024]{2,1,0:T(8,128)(2,1)} custom-call(s32[16,48]{1,0:T(8,128)} %bitcast.6, s32[16,48]{1,0:T(8,128)} %bitcast.7, s32[16]{0:T(128)} %bitcast.9, s32[16,48,2048]{2,1,0:T(8,128)} %bitcast.5), custom_call_target="tpu_custom_call" | custom-call | flops 50000000 | bytes 40000000 | tf_op jit(solution)/shard_map/pallas_call | solution.py:70
  19.3 132.8 %shard_map.104 = (f32[256,128]{1,0:T(8,128)}, f32[256,128]{1,0:T(8,128)}, f32[128,128]{1,0:T(8,128)}) custom-call(f32[256,128]{1,0:T(8,128)} %features.1, f32[1,256]{1,0:T(1,128)} %bitcast.8, bf16[128,128]{1,0:T(8,128)(2,1)} %weight.1, f32[256,128]{1,0:T(8,128)} %cotangent.1, bf16[16,1024,1024]{2,1,0:T(8,128)(2,1)} %shard_map.103.dense), custom_call_target="tpu_custom_call" | custom-call | flops 8999999488 | bytes 34000000 | tf_op jit(solution)/shard_map/pallas_call | solution.py:569
  152.1 1.7 %shard_map.105 = (f32[256,128]{1,0:T(8,128)}, f32[256,128]{1,0:T(8,128)}, f32[128,128]{1,0:T(8,128)}) custom-call(f32[256,128]{1,0:T(8,128)} %get-tuple-element.6.act, f32[256,128]{1,0:T(8,128)} %get-tuple-element.7.feature_grad, f32[128,128]{1,0:T(8,128)} %get-tuple-element.8.weight_grad), custom_call_target="tpu_custom_call" | custom-call | bytes 640000 | tf_op jit(solution)/shard_map/pallas_call | solution.py:556

commit v4 on v3

--- a/solution.py
+++ b/solution.py
@@ -15,40 +15,49 @@
 UNROLL = 4
 WIDE = 512
 LAG = 3
-PAIR = 2
 MESH = pl.DeviceIdType.MESH
 
 
-def dense_kernel(rows, cols, counts, words, out, packed):
+def dense_kernel(rows, cols, counts, masks, out, words, packed, sem):
     lane = lax.broadcasted_iota(jnp.int32, (8, 128), 1)
     row = lax.broadcasted_iota(jnp.int32, (8, 128), 0)
     place = row * 16 + lax.rem(lane, 16)
     bit = lax.div(lane, 16)
-    out[...] = jnp.zeros_like(out)
-    for which in range(PAIR):
-        packed[which, pl.ds(CAP, UNROLL)] = jnp.zeros((UNROLL, 4, 128), jnp.int32)
+
+    def fetch(section, held):
+        return pltpu.make_async_copy(masks.at[section], words.at[held], sem.at[held])
+
+    fetch(0, 0).start()
+    packed[pl.ds(CAP, UNROLL)] = jnp.zeros((UNROLL, 4, 128), jnp.int32)
+
+    def near_of(group):
+        return [
+            jnp.take_along_axis(
+                jnp.broadcast_to(packed[group * UNROLL + index, pl.ds(part, 1), :], (8, 128)),
+                place, axis=1, mode="promise_in_bounds",
+            )
+            for index in range(UNROLL) for part in range(4)
+        ]
+
+    def section_step(section, carry):
+        held = section % 2
+
+        @pl.when(section + 1 < SECTIONS)
+        def _():
+            fetch(section + 1, (section + 1) % 2).start()
+
+        out[section] = jnp.zeros((STRIPE, STRIPE), jnp.bfloat16)
+        fetch(section, held).wait()
         for eight in range(CAP // 8):
             slots = pl.ds(eight * 8, 8)
             for part in range(4):
-                value = words[which, slots, pl.ds(part * 512, 128)]
+                value = words[held, slots, pl.ds(part * 512, 128)]
                 for step in range(1, 4):
-                    value = value | (words[which, slots, pl.ds(part * 512 + step * 128, 128)] << (8 * step))
-                packed[which, slots, part, :] = value
-
-    for which in range(PAIR):
-        section = pl.program_id(0) * PAIR + which
+                    value = value | (words[held, slots, pl.ds(part * 512 + step * 128, 128)] << (8 * step))
+                packed[slots, part, :] = value
         live_count = counts[section]
 
-        def near_of(group, which=which):
-            return [
-                jnp.take_along_axis(
-                    jnp.broadcast_to(packed[which, group * UNROLL + index, pl.ds(part, 1), :], (8, 128)),
-                    place, axis=1, mode="promise_in_bounds",
-                )
-                for index in range(UNROLL) for part in range(4)
-            ]
-
-        def group_step(group, nears, which=which, section=section, live_count=live_count, near_of=near_of):
+        def group_step(group, nears):
             later = near_of(group + 1)
             for index in range(UNROLL):
                 slot = group * UNROLL + index
@@ -60,33 +69,37 @@
                 tile = jnp.concatenate(strips, axis=0).astype(jnp.bfloat16)
                 top = pl.multiple_of(rows[section, slot] * TILE, TILE)
                 left = pl.multiple_of(cols[section, slot] * TILE, TILE)
-                out[which, pl.ds(top, TILE), pl.ds(left, TILE)] += tile
+                out[section, pl.ds(top, TILE), pl.ds(left, TILE)] += tile
             return later
 
         lax.fori_loop(0, (live_count + UNROLL - 1) // UNROLL, group_step, near_of(0))
+        return carry
+
+    lax.fori_loop(0, SECTIONS, section_step, 0)
 
 
 def dense_blocks(tile_rows, tile_cols, tile_counts, tile_masks):
+    smem = pl.BlockSpec(memory_space=pltpu.SMEM)
     return pl.pallas_call(
         dense_kernel,
-        out_shape=jax.ShapeDtypeStruct((SECTIONS, STRIPE, STRIPE), jnp.bfloat16),
-        grid_spec=pltpu.PrefetchScalarGridSpec(
-            num_scalar_prefetch=3,
-            grid=(SECTIONS // PAIR,),
-            in_specs=[pl.BlockSpec((PAIR, CAP, 2048), lambda k, *_: (k, 0, 0))],
-            out_specs=pl.BlockSpec((PAIR, STRIPE, STRIPE), lambda k, *_: (k, 0, 0)),
-            scratch_shapes=[pltpu.VMEM((PAIR, CAP + UNROLL, 4, 128), jnp.int32)],
-        ),
-        compiler_params=pltpu.CompilerParams(vmem_limit_bytes=60 * 1024 * 1024),
-        cost_estimate=pl.CostEstimate(flops=50_000_000, bytes_accessed=40_000_000, transcendentals=0),
+        out_shape=pltpu.VMEM((SECTIONS, STRIPE, STRIPE), jnp.bfloat16),
+        in_specs=[smem, smem, smem, pl.BlockSpec(memory_space=pl.ANY)],
+        out_specs=pl.BlockSpec(memory_space=pltpu.VMEM),
+        scratch_shapes=[
+            pltpu.VMEM((2, CAP, 2048), jnp.int32),
+            pltpu.VMEM((CAP + UNROLL, 4, 128), jnp.int32),
+            pltpu.SemaphoreType.DMA((2,)),
+        ],
+        compiler_params=pltpu.CompilerParams(vmem_limit_bytes=28 * 1024 * 1024),
+        cost_estimate=pl.CostEstimate(flops=50_000_000, bytes_accessed=8_000_000, transcendentals=0),
     )(tile_rows, tile_cols, tile_counts, tile_masks)
 
 
 def layer_kernel(
-    features, norm, weight, cotangent, dense, act, feature_grad, weight_grad,
-    blocks, stripes, own, mate, mate_out, mate_in, totals, parting, parts, pushed, own_pushed, sums, going, going_thin, coming, coming_thin, coming_low,
+    features, norm, weight, cotangent, blocks, act, feature_grad, weight_grad,
+    stripes, own, mate, mate_out, mate_in, totals, parting, parts, pushed, own_pushed, sums, going, going_thin, coming, coming_thin, coming_low,
     coming_thin_low, given, taken, shares, shared, terms, other_terms,
-    dense_sem, mate_send, mate_recv, mate_back_send, mate_back_recv, team_send, team_recv, ring_send, ring_send_low, ring_recv, thin_send, thin_send_low, thin_recv, peer_send,
+    mate_send, mate_recv, mate_back_send, mate_back_recv, team_send, team_recv, ring_send, ring_send_low, ring_recv, thin_send, thin_send_low, thin_recv, peer_send,
     peer_recv, part_send, part_recv, push_send, push_recv, back_send, back_recv, back_recv_low, back_thin_send,
     back_thin_recv, back_thin_recv_low, give_send, give_recv, share_send, share_recv, term_send, term_recv,
 ):
@@ -124,8 +137,8 @@
 
     before = [(depth + 4 - offset) % 4 for offset in range(1, 4)]
     partners = [
-        (loop, toggled(depth, 1)), (loop, toggled(depth, 2)), (toggled(loop, 4), depth), (toggled(loop, 1), depth),
-        (toggled(loop, 2), depth), (toggled(loop, 8), depth), (toggled(loop, 16), depth), (toggled(loop, 32), depth),
+        (toggled(loop, 32), depth), (toggled(loop, 16), depth), (toggled(loop, 8), depth), (toggled(loop, 2), depth),
+        (toggled(loop, 1), depth), (toggled(loop, 4), depth), (loop, toggled(depth, 2)), (loop, toggled(depth, 1)),
     ]
 
     def section_of(slot):
@@ -139,17 +152,8 @@
         passes = (index >= 2) & ((distance < 3) | ((distance == 3) & (other == up)))
         return distance, up, other, slot, passes
 
-    def load_of(section):
-        return pltpu.make_async_copy(dense.at[section], blocks.at[section], dense_sem.at[section])
-
-    def load_step(index, carry):
-        load_of(section_of(step_of(index)[3])).start()
-        return carry
-
-    lax.fori_loop(0, SECTIONS, load_step, 0)
-
     barrier = pltpu.get_barrier_semaphore()
-    for device in [above, below] + beside + [peer_device((depth + offset) % 4) for offset in range(1, 4)] + [mate_device, partners[3], partners[4], partners[6], partners[7]]:
+    for device in [above, below] + beside + [peer_device((depth + offset) % 4) for offset in range(1, 4)] + [mate_device, partners[0], partners[1], partners[3], partners[4]]:
         pl.semaphore_signal(barrier, inc=1, device_id=device, device_id_type=MESH)
     for index in range(4):
         def greet(index=index):
@@ -293,7 +297,6 @@
                 peer_copy(slot, far, 0, near).wait_recv()
                 peer_copy(slot, two, 0, near).wait_recv()
 
-            load_of(section).wait()
             totals[...] += jnp.dot(blocks[section], stripes[slot], preferred_element_type=jnp.float32)
 
         return carry
@@ -389,7 +392,57 @@
         given[slot, 1] = (sums[held, :, lanes_of(near)] + taken[slot, 0].astype(jnp.float32)).astype(jnp.bfloat16)
         give_copy(slot, 1, near).start()
 
-    def reduce(index, held):
+    def share(other, held, pieces):
+        for piece in pieces:
+            shares[other, piece] = sums[held, :, pl.ds(piece * PIECE, PIECE)].astype(jnp.bfloat16)
+            if piece == 0:
+                @pl.when(jnp.logical_not(first))
+                def _():
+                    share_copy(other, 0).start()
+
+                @pl.when(first)
+                def _():
+                    shared[other, 0] = shares[other, 0]
+            else:
+                share_copy(other, piece).start()
+
+    def send_back(index, copy, main, low):
+        distance, up, other, slot, passes = step_of(index)
+        last_far = distance == 4
+
+        @pl.when((index >= 2) & (((up == 0) & jnp.logical_not(last_far)) | (last_far & (other == 0))))
+        def _():
+            copy(slot, main[0].at[slot], main[1].at[slot], below).start()
+
+        @pl.when((index >= 2) & (((up == 1) & (distance > 1)) | (last_far & (other == 1))))
+        def _():
+            copy(slot, main[0].at[slot], main[1].at[slot], above).start()
+
+        @pl.when((index >= 2) & (up == 1) & (distance == 1))
+        def _():
+            copy(slot, low[0].at[other], low[1].at[other], above).start()
+
+    def reduce_wide(index, held):
+        distance, up, other, slot, passes = step_of(index)
+
+        @pl.when(passes | (index < 2))
+        def _():
+            back_copy(slot, coming.at[slot], back_recv.at[slot], above).wait_recv()
+            sums[held, :, wide] += coming[slot].astype(jnp.float32)
+
+        @pl.when(index < 2)
+        def _():
+            back_copy(slot, coming_low.at[other], back_recv_low.at[other], below).wait_recv()
+            sums[held, :, wide] += coming_low[other].astype(jnp.float32)
+            share(other, held, (0, 1))
+
+        @pl.when(index >= 2)
+        def _():
+            going[slot] = sums[held, :, wide].astype(jnp.bfloat16)
+
+        send_back(index, back_copy, (coming, back_recv), (coming_low, back_recv_low))
+
+    def reduce_thin(index, held):
         distance, up, other, slot, passes = step_of(index)
 
         @pl.when(index >= 2)
@@ -403,65 +456,38 @@
         def _():
             back_thin_copy(slot, coming_thin.at[slot], back_thin_recv.at[slot], above).wait_recv()
             sums[held, :, thin] += coming_thin[slot].astype(jnp.float32)
-            back_copy(slot, coming.at[slot], back_recv.at[slot], above).wait_recv()
-            sums[held, :, wide] += coming[slot].astype(jnp.float32)
 
         @pl.when(index < 2)
         def _():
             back_thin_copy(slot, coming_thin_low.at[other], back_thin_recv_low.at[other], below).wait_recv()
             sums[held, :, thin] += coming_thin_low[other].astype(jnp.float32)
-            back_copy(slot, coming_low.at[other], back_recv_low.at[other], below).wait_recv()
-            sums[held, :, wide] += coming_low[other].astype(jnp.float32)
-            for piece in range(4):
-                shares[other, piece] = sums[held, :, pl.ds(piece * PIECE, PIECE)].astype(jnp.bfloat16)
-                if piece == 0:
-                    @pl.when(jnp.logical_not(first))
-                    def _():
-                        share_copy(other, 0).start()
-
-                    @pl.when(first)
-                    def _():
-                        shared[other, 0] = shares[other, 0]
-                else:
-                    share_copy(other, piece).start()
+            share(other, held, (2, 3))
 
         @pl.when(index >= 2)
         def _():
             going_thin[slot] = sums[held, :, thin].astype(jnp.bfloat16)
-            going[slot] = sums[held, :, wide].astype(jnp.bfloat16)
-
-        last_far = distance == 4
-
-        @pl.when((index >= 2) & (((up == 0) & jnp.logical_not(last_far)) | (last_far & (other == 0))))
-        def _():
-            back_thin_copy(slot, coming_thin.at[slot], back_thin_recv.at[slot], below).start()
-            back_copy(slot, coming.at[slot], back_recv.at[slot], below).start()
-
-        @pl.when((index >= 2) & (((up == 1) & (distance > 1)) | (last_far & (other == 1))))
-        def _():
-            back_thin_copy(slot, coming_thin.at[slot], back_thin_recv.at[slot], above).start()
-            back_copy(slot, coming.at[slot], back_recv.at[slot], above).start()
-
-        @pl.when((index >= 2) & (up == 1) & (distance == 1))
-        def _():
-            back_thin_copy(slot, coming_thin_low.at[other], back_thin_recv_low.at[other], above).start()
-            back_copy(slot, coming_low.at[other], back_recv_low.at[other], above).start()
+
+        send_back(index, back_thin_copy, (coming_thin, back_thin_recv), (coming_thin_low, back_thin_recv_low))
 
     def backward_step(count, carry):
         @pl.when(count < SECTIONS)
         def _():
             multiply(SECTIONS - 1 - count, count % (LAG + 1))
 
-        @pl.when((count >= 1) & (count < SECTIONS - 1))
-        def _():
-            hand_on(SECTIONS - count, (count - 1) % (LAG + 1))
+        @pl.when((count >= 1) & (count < SECTIONS + 1))
+        def _():
+            reduce_wide(SECTIONS - count, (count - 1) % (LAG + 1))
+
+        @pl.when((count >= 2) & (count < SECTIONS))
+        def _():
+            hand_on(SECTIONS + 1 - count, (count - 2) % (LAG + 1))
 
         @pl.when(count >= LAG)
         def _():
-            reduce(SECTIONS - 1 - (count - LAG), (count - LAG) % (LAG + 1))
+            reduce_thin(SECTIONS - 1 - (count - LAG), (count - LAG) % (LAG + 1))
 
         for step in range(1, 8):
-            @pl.when(count == 2 * step)
+            @pl.when(count == (2, 4, 6, 9, 12, 15, 18)[step - 1])
             def _(step=step):
                 term_copy(step - 1).wait_recv()
                 terms[step] = terms[step - 1] + other_terms[step - 1]
@@ -558,6 +584,7 @@
         out_shape=tuple(jax.ShapeDtypeStruct(value.shape, value.dtype) for value in results),
         in_specs=[vmem] * 3,
         out_specs=(vmem,) * 3,
+        compiler_params=pltpu.CompilerParams(vmem_limit_bytes=60 * 1024 * 1024),
         cost_estimate=pl.CostEstimate(flops=0, bytes_accessed=640_000, transcendentals=0),
     )(*results)
 
@@ -573,10 +600,9 @@
             jax.ShapeDtypeStruct((PIECE, FEAT), f32),
             jax.ShapeDtypeStruct((FEAT, FEAT), f32),
         ),
-        in_specs=[vmem, vmem, vmem, vmem, pl.BlockSpec(memory_space=pl.ANY)],
+        in_specs=[vmem, vmem, vmem, vmem, vmem],
         out_specs=(vmem, vmem, vmem),
         scratch_shapes=[
-            pltpu.VMEM((SECTIONS, STRIPE, STRIPE), bf16),
             pltpu.VMEM((SECTIONS, STRIPE, FEAT), bf16),
             pltpu.VMEM((PIECE, FEAT), bf16),
             pltpu.VMEM((PIECE, FEAT), bf16),
@@ -600,7 +626,7 @@
             pltpu.VMEM((2, 4, FEAT, PIECE), bf16),
             pltpu.VMEM((8, FEAT, FEAT), f32),
             pltpu.VMEM((8, FEAT, FEAT), f32),
-            dma((SECTIONS,)), dma, dma, dma, dma,
+            dma, dma, dma, dma,
             dma((2, 4)), dma((2, 4)), dma((SECTIONS,)), dma((2,)), dma((SECTIONS,)),
             dma((SECTIONS,)), dma((2,)), dma((SECTIONS,)), dma((SECTIONS, 3)), dma((SECTIONS, 4)),
             dma((3,)), dma((3,)), dma((3,)), dma((3,)),
@@ -609,10 +635,10 @@
             dma((2, 4)), dma((2, 4)), dma((8,)), dma((8,)),
         ],
         compiler_params=pltpu.CompilerParams(
-            collective_id=0, has_side_effects=True, vmem_limit_bytes=60 * 1024 * 1024
+            collective_id=0, has_side_effects=True, vmem_limit_bytes=30 * 1024 * 1024
         ),
         cost_estimate=pl.CostEstimate(flops=9_000_000_000, bytes_accessed=34_000_000, transcendentals=32768),
-    )(features, norm_row, weight, cotangent, dense)
+    )(features, norm_row, weight, cotangent, pltpu.with_memory_space_constraint(dense, pltpu.VMEM))
 
 
 def per_device(features, norm_scale, weight, cotangent, tile_rows, tile_cols, tile_masks, tile_counts):

time: 154 us -> 148 us (0.961)
  Pallas kernels: 153 us -> 147 us
    pallas_call x1, Pallas kernels: 18.7 us -> 12.4 us  [dense_blocks(): pl.pallas_call(dense_kernel, out_shape=pltpu.VMEM((SECTIONS, STRIPE, STRI...]
where the time goes in v4:
time: 148 us; the launch traced here: 147 us
  Pallas kernels  147 us (99%)
    pallas_call x1, Pallas kernels, layer(): pl.pallas_call(layer_kernel, out_shape=(jax.ShapeDtypeStruct((PIECE, FEAT...  133 us
    pallas_call x1, Pallas kernels, dense_blocks(): pl.pallas_call(dense_kernel, out_shape=pltpu.VMEM((SECTIONS, STRIPE, STRI...  12.4 us

profile of v4, /device:TPU:1, one launch (start us, length us, event | category | flops | bytes accessed | tf_op | source)
XLA Modules:
  0.0 147.3 jit_solution(12865603361711131646)
XLA Ops:
  0.6 12.4 %shard_map.103.blocks = bf16[16,1024,1024]{2,1,0:T(8,128)(2,1)S(1)} custom-call(s32[16,48]{1,0:T(8,128)} %bitcast.6, s32[16,48]{1,0:T(8,128)} %bitcast.7, s32[16]{0:T(128)} %bitcast.9, s32[16,48,2048]{2,1,0:T(8,128)} %bitcast.5), custom_call_target="tpu_custom_call" | custom-call | flops 50000000 | bytes 8000000 | tf_op jit(solution)/shard_map/pallas_call | solution.py:83
  13.0 132.5 %shard_map.104 = (f32[256,128]{1,0:T(8,128)}, f32[256,128]{1,0:T(8,128)}, f32[128,128]{1,0:T(8,128)}) custom-call(f32[256,128]{1,0:T(8,128)} %features.1, f32[1,256]{1,0:T(1,128)} %bitcast.8, bf16[128,128]{1,0:T(8,128)(2,1)} %weight.1, f32[256,128]{1,0:T(8,128)} %cotangent.1, bf16[16,1024,1024]{2,1,0:T(8,128)(2,1)S(1)} %shard_map.103.blocks), custom_call_target="tpu_custom_call" | custom-call | flops 8999999488 | bytes 34000000 | tf_op jit(solution)/shard_map/pallas_call | solution.py:596
  145.6 1.7 %shard_map.105 = (f32[256,128]{1,0:T(8,128)}, f32[256,128]{1,0:T(8,128)}, f32[128,128]{1,0:T(8,128)}) custom-call(f32[256,128]{1,0:T(8,128)} %get-tuple-element.6.act, f32[256,128]{1,0:T(8,128)} %get-tuple-element.7.feature_grad, f32[128,128]{1,0:T(8,128)} %get-tuple-element.8.weight_grad), custom_call_target="tpu_custom_call" | custom-call | bytes 640000 | tf_op jit(solution)/shard_map/pallas_call | solution.py:582

commit v5 on v4

--- a/solution.py
+++ b/solution.py
@@ -14,7 +14,7 @@
 RING = 8
 UNROLL = 4
 WIDE = 512
-LAG = 3
+LAG = 4
 MESH = pl.DeviceIdType.MESH
 
 
@@ -277,17 +277,17 @@
         def _():
             pass_on(count)
 
-        @pl.when((count >= 3) & (count < SECTIONS + 1))
-        def _():
-            distance, up, other, slot, passes = step_of(count - 1)
+        @pl.when((count >= 4) & (count < SECTIONS + 2))
+        def _():
+            distance, up, other, slot, passes = step_of(count - 2)
             near, far = around(other)
             relay = peer_copy(slot, near, 2, far)
             relay.wait_recv()
             relay.start()
 
-        @pl.when(count >= LAG)
-        def _():
-            index = count - LAG
+        @pl.when((count == 1) | (count == 2) | (count >= LAG + 2))
+        def _():
+            index = count - jnp.where(count < LAG, 1, LAG)
             distance, up, other, slot, passes = step_of(index)
             section = section_of(slot)
 

time: 148 us -> 141 us (0.953)
  Pallas kernels: 147 us -> 140 us
    pallas_call x1, Pallas kernels: 133 us -> 121 us  [layer(): pl.pallas_call(layer_kernel, out_shape=(jax.ShapeDtypeStruct((PIECE, FEAT...]
    pallas_call x1, Pallas kernels: 12.4 us -> 17.5 us  [dense_blocks(): pl.pallas_call(dense_kernel, out_shape=pltpu.VMEM((SECTIONS, STRIPE, STRI...]
where the time goes in v5:
time: 141 us
  Pallas kernels  140 us (99%)
    pallas_call x1, Pallas kernels, layer(): pl.pallas_call(layer_kernel, out_shape=(jax.ShapeDtypeStruct((PIECE, FEAT...  121 us
    pallas_call x1, Pallas kernels, dense_blocks(): pl.pallas_call(dense_kernel, out_shape=pltpu.VMEM((SECTIONS, STRIPE, STRI...  17.5 us

profile of v5, /device:TPU:1, one launch (start us, length us, event | category | flops | bytes accessed | tf_op | source)
XLA Modules:
  0.0 140.9 jit_solution(16499285369976303775)
XLA Ops:
  0.6 17.5 %shard_map.103.blocks = bf16[16,1024,1024]{2,1,0:T(8,128)(2,1)S(1)} custom-call(s32[16,48]{1,0:T(8,128)} %bitcast.6, s32[16,48]{1,0:T(8,128)} %bitcast.7, s32[16]{0:T(128)} %bitcast.9, s32[16,48,2048]{2,1,0:T(8,128)} %bitcast.5), custom_call_target="tpu_custom_call" | custom-call | flops 50000000 | bytes 8000000 | tf_op jit(solution)/shard_map/pallas_call | solution.py:83
  18.1 121.1 %shard_map.104 = (f32[256,128]{1,0:T(8,128)}, f32[256,128]{1,0:T(8,128)}, f32[128,128]{1,0:T(8,128)}) custom-call(f32[256,128]{1,0:T(8,128)} %features.1, f32[1,256]{1,0:T(1,128)} %bitcast.8, bf16[128,128]{1,0:T(8,128)(2,1)} %weight.1, f32[256,128]{1,0:T(8,128)} %cotangent.1, bf16[16,1024,1024]{2,1,0:T(8,128)(2,1)S(1)} %shard_map.103.blocks), custom_call_target="tpu_custom_call" | custom-call | flops 8999999488 | bytes 34000000 | tf_op jit(solution)/shard_map/pallas_call | solution.py:596
  139.2 1.7 %shard_map.105 = (f32[256,128]{1,0:T(8,128)}, f32[256,128]{1,0:T(8,128)}, f32[128,128]{1,0:T(8,128)}) custom-call(f32[256,128]{1,0:T(8,128)} %get-tuple-element.6.act, f32[256,128]{1,0:T(8,128)} %get-tuple-element.7.feature_grad, f32[128,128]{1,0:T(8,128)} %get-tuple-element.8.weight_grad), custom_call_target="tpu_custom_call" | custom-call | bytes 640000 | tf_op jit(solution)/shard_map/pallas_call | solution.py:582

commit v6 on v5

--- a/solution.py
+++ b/solution.py
@@ -375,7 +375,12 @@
 
     def multiply(index, held):
         distance, up, other, slot, passes = step_of(index)
-        sums[held] = jnp.dot(pushed[...], blocks[section_of(slot)], preferred_element_type=jnp.float32)
+        section = section_of(slot)
+        for part in range(4):
+            lanes = pl.ds(part * 256, 256)
+            sums[held, :, lanes] = jnp.dot(
+                pushed[...], blocks[section, :, lanes], preferred_element_type=jnp.float32
+            )
 
         @pl.when(index >= 2)
         def _():

time: 141 us -> 144 us (1.021)
  Pallas kernels: 140 us -> 143 us
    pallas_call x1, Pallas kernels: 121 us -> 124 us  [layer(): pl.pallas_call(layer_kernel, out_shape=(jax.ShapeDtypeStruct((PIECE, FEAT...]
where the time goes in v6:
time: 144 us
  Pallas kernels  143 us (99%)
    pallas_call x1, Pallas kernels, layer(): pl.pallas_call(layer_kernel, out_shape=(jax.ShapeDtypeStruct((PIECE, FEAT...  124 us
    pallas_call x1, Pallas kernels, dense_blocks(): pl.pallas_call(dense_kernel, out_shape=pltpu.VMEM((SECTIONS, STRIPE, STRI...  17.6 us

profile of v6, /device:TPU:1, one launch (start us, length us, event | category | flops | bytes accessed | tf_op | source)
XLA Modules:
  0.0 144.1 jit_solution(1343036375998247116)
XLA Ops:
  0.6 17.6 %shard_map.103.blocks = bf16[16,1024,1024]{2,1,0:T(8,128)(2,1)S(1)} custom-call(s32[16,48]{1,0:T(8,128)} %bitcast.6, s32[16,48]{1,0:T(8,128)} %bitcast.7, s32[16]{0:T(128)} %bitcast.9, s32[16,48,2048]{2,1,0:T(8,128)} %bitcast.5), custom_call_target="tpu_custom_call" | custom-call | flops 50000000 | bytes 8000000 | tf_op jit(solution)/shard_map/pallas_call | solution.py:83
  18.3 124.1 %shard_map.104 = (f32[256,128]{1,0:T(8,128)}, f32[256,128]{1,0:T(8,128)}, f32[128,128]{1,0:T(8,128)}) custom-call(f32[256,128]{1,0:T(8,128)} %features.1, f32[1,256]{1,0:T(1,128)} %bitcast.8, bf16[128,128]{1,0:T(8,128)(2,1)} %weight.1, f32[256,128]{1,0:T(8,128)} %cotangent.1, bf16[16,1024,1024]{2,1,0:T(8,128)(2,1)S(1)} %shard_map.103.blocks), custom_call_target="tpu_custom_call" | custom-call | flops 8999999488 | bytes 34000000 | tf_op jit(solution)/shard_map/pallas_call | solution.py:601
  142.4 1.7 %shard_map.105 = (f32[256,128]{1,0:T(8,128)}, f32[256,128]{1,0:T(8,128)}, f32[128,128]{1,0:T(8,128)}) custom-call(f32[256,128]{1,0:T(8,128)} %get-tuple-element.6.act, f32[256,128]{1,0:T(8,128)} %get-tuple-element.7.feature_grad, f32[128,128]{1,0:T(8,128)} %get-tuple-element.8.weight_grad), custom_call_target="tpu_custom_call" | custom-call | bytes 640000 | tf_op jit(solution)/shard_map/pallas_call | solution.py:587
